TPU v7x, 512 devices: a whole 4x8x8 slice. The times are simulated.
512 devices in a mesh: patch: 4 (over x), curve: 128 (over z, y, core).
Axes of the slice: x: 4, y: 8, z: 8, core: 2. Of those that a mesh axis runs over, the one named last changes fastest.
Arguments:
- points: bfloat16 [128, 4, 256, 512], P('curve', 'patch'), may hold values from -6 to 6
- norm_gain_one: float32 [512], replicated, may hold values from 0.4 to 2.5, as said below
- qkv_one: bfloat16 [512, 1536], replicated, may hold values from -0.25 to 0.25
- out_one: bfloat16 [512, 512], replicated, may hold values from -0.25 to 0.25
- hilbert_pos: int32 [128, 4, 256], P('curve', 'patch'), may hold values from 0 to 32767, as said below
- norm_gain_two: float32 [512], replicated, may hold values from 0.4 to 2.5, as said below
- qkv_two: bfloat16 [512, 1536], replicated, may hold values from -0.25 to 0.25
- out_two: bfloat16 [512, 512], replicated, may hold values from -0.25 to 0.25
- hilbert_seg: int32 [4, 128, 256], P('patch', 'curve'), may hold values from 0 to 7, never falling along the last dimension, each value on 1 to 128 neighbouring positions
- out_grad: bfloat16 [4, 128, 256, 512], P('patch', 'curve'), may hold values from -6 to 6
Outputs:
- point_grad: bfloat16 [128, 4, 256, 512], P('curve', 'patch')
Inputs may be any that keep to these rules, and one draw needn't show every extreme that they name: `hilbert_pos`: for each index p of the second dimension, the values over all c and i form a permutation of 0 to 32767. From the points of one device at most 4 have q // 256 equal to any one value, and in every draw some device sends exactly 4 to some owner. `hilbert_seg`: within one device's slots the numbers never fall; a patch holds at most 128 slots. `norm_gain_one`: positive gains. `norm_gain_two`: positive gains.
All inputs are finite; a program needn't handle non-finite values.
Results may differ from a plain program's by a relative error of at most 0.02.
Values may be sent and summed in bfloat16 or wider, within the bound.
A program may use at most 64 MiB of HBM per device.

v0:
```python
import jax
import jax.numpy as jnp
from jax import lax
from jax.sharding import PartitionSpec as P

HEADS = 16


EPS = 1e-06


def prepare(source_rows, gain, w_qkv):
    wide = source_rows.astype(jnp.float32)
    power = jnp.mean(wide * wide, axis=-1, keepdims=True)
    normed = (wide * lax.rsqrt(power + EPS) * gain).astype(jnp.bfloat16)
    return jnp.dot(normed, w_qkv, preferred_element_type=jnp.float32).astype(jnp.bfloat16)


def finish(source_rows, mixed, w_out):
    total = source_rows.astype(jnp.float32) + jnp.dot(
        mixed, w_out, preferred_element_type=jnp.float32
    )
    return total.astype(jnp.bfloat16)


def attend(queries, keys, values, allowed):
    count, width = queries.shape
    depth = width // HEADS
    q_heads = queries.astype(jnp.float32).reshape(count, HEADS, depth)
    k_heads = keys.astype(jnp.float32).reshape(-1, HEADS, depth)
    v_heads = values.astype(jnp.float32).reshape(-1, HEADS, depth)
    scores = jnp.einsum("rhe,khe->hrk", q_heads, k_heads) * depth ** (-0.5)
    scores = jnp.where(allowed[None], scores, -1e30)
    weights = jax.nn.softmax(scores, axis=-1)
    rounded = lax.optimization_barrier(weights.astype(jnp.bfloat16))
    mixed = jnp.einsum("hrk,khe->rhe", rounded.astype(jnp.float32), v_heads)
    return mixed.reshape(count, width).astype(jnp.bfloat16)


def device_block(source_rows, segment, gain, w_qkv, w_out):
    width = source_rows.shape[1]
    packed = prepare(source_rows, gain, w_qkv)
    allowed = segment[:, None] == segment[None, :]
    mixed = attend(packed[:, :width], packed[:, width : 2 * width], packed[:, 2 * width :], allowed)
    return finish(source_rows, mixed, w_out)


def head_view(matrix, index, block, depth):
    columns = block * depth
    piece = lax.dynamic_slice_in_dim(matrix, index * columns, columns, 1)
    return piece.reshape(matrix.shape[0], block, depth)


def regroup(stacked):
    groups, length, columns = stacked.shape
    return jnp.transpose(stacked, (1, 0, 2)).reshape(length, groups * columns)


def round_trip(values):
    return lax.optimization_barrier(values.astype(jnp.bfloat16)).astype(jnp.float32)


def shards(
    points,
    norm_gain_one,
    qkv_one,
    out_one,
    hilbert_pos,
    norm_gain_two,
    qkv_two,
    out_two,
    hilbert_seg,
    out_grad,
):
    count = points.shape[2]
    width = points.shape[3]
    depth = width // HEADS
    block = 4
    groups = HEADS // block
    scale = depth ** (-0.5)
    source_rows = points.reshape(count, width)
    packed, prep_pull = jax.vjp(lambda inputs: prepare(inputs, norm_gain_one, qkv_one), source_rows)
    queries = packed[:, :width]
    gathered = lax.all_gather(packed[:, width:], "patch", axis=0, tiled=True)
    keys_all = gathered[:, :width]
    values_all = gathered[:, width:]
    patch_len = gathered.shape[0]

    def forward_group(index):
        q_part = head_view(queries, index, block, depth)
        k_part = head_view(keys_all, index, block, depth)
        v_part = head_view(values_all, index, block, depth)
        scores = (
            jnp.einsum("rhe,khe->hrk", q_part, k_part, preferred_element_type=jnp.float32) * scale
        )
        weights = jax.nn.softmax(scores, axis=-1).astype(jnp.bfloat16)
        mixed_part = jnp.einsum("hrk,khe->rhe", weights, v_part, preferred_element_type=jnp.float32)
        return mixed_part.reshape(count, block * depth)

    mixed = regroup(lax.map(forward_group, jnp.arange(groups))).astype(jnp.bfloat16)
    moved, finish_pull = jax.vjp(
        lambda inputs, mix: finish(inputs, mix, out_one), source_rows, mixed
    )
    curve_size = lax.axis_size("curve")
    capacity = 2 * count // curve_size
    target = hilbert_pos.reshape(count)
    owner = target // count
    offset = target % count
    columns = jnp.arange(curve_size, dtype=jnp.int32)
    onehot = (owner[:, None] == columns[None, :]).astype(jnp.bfloat16)
    earlier = (
        lax.broadcasted_iota(jnp.int32, (count, count), 0)
        > lax.broadcasted_iota(jnp.int32, (count, count), 1)
    ).astype(jnp.bfloat16)
    before = jnp.dot(earlier, onehot, preferred_element_type=jnp.float32)
    ranking = jnp.sum(before * onehot.astype(jnp.float32), axis=1).astype(jnp.int32)
    slot = owner * capacity + ranking
    outgoing = jnp.zeros((curve_size * capacity, width), jnp.bfloat16).at[slot].set(moved)
    outgoing_at = jnp.full((curve_size * capacity,), count, jnp.int32).at[slot].set(offset)
    arrived, arrived_at = (
        lax.all_to_all(
            outgoing.reshape(curve_size, capacity, width),
            "curve",
            split_axis=0,
            concat_axis=0,
            tiled=True,
        ),
        lax.all_to_all(
            outgoing_at.reshape(curve_size, capacity),
            "curve",
            split_axis=0,
            concat_axis=0,
            tiled=True,
        ),
    )
    landing = arrived_at.reshape(-1)
    hilbert_rows = (
        jnp.zeros((count, width), jnp.bfloat16)
        .at[landing]
        .set(arrived.reshape(-1, width), mode="drop")
    )
    segment = hilbert_seg.reshape(count)
    _, second_pull = jax.vjp(
        lambda inputs: device_block(inputs, segment, norm_gain_two, qkv_two, out_two), hilbert_rows
    )
    (hilbert_grad,) = second_pull(out_grad.reshape(count, width))
    valid = landing < count
    clipped = jnp.minimum(landing, count - 1)
    returning = jnp.where(
        valid[:, None], jnp.take(hilbert_grad, clipped, axis=0), jnp.zeros((), jnp.bfloat16)
    )
    arrived_home = lax.all_to_all(
        returning.reshape(curve_size, capacity, width),
        "curve",
        split_axis=0,
        concat_axis=0,
        tiled=True,
    )
    moved_grad = arrived_home.reshape(-1, width)[slot]
    residual_grad, mixed_grad = finish_pull(moved_grad)

    def backward_group(index):
        q_part = head_view(queries, index, block, depth)
        k_part = head_view(keys_all, index, block, depth)
        v_part = head_view(values_all, index, block, depth)
        g_part = head_view(mixed_grad, index, block, depth)
        scores = (
            jnp.einsum("rhe,khe->hrk", q_part, k_part, preferred_element_type=jnp.float32) * scale
        )
        weights = jax.nn.softmax(scores, axis=-1)
        rounded = weights.astype(jnp.bfloat16)
        weight_grad = round_trip(
            jnp.einsum("rhe,khe->hrk", g_part, v_part, preferred_element_type=jnp.float32)
        )
        score_grad = (
            weights * (weight_grad - jnp.sum(weights * weight_grad, axis=-1, keepdims=True)) * scale
        )
        query_grad = jnp.einsum("hrk,khe->rhe", score_grad, k_part.astype(jnp.float32)).reshape(
            count, block * depth
        )
        key_grad = jnp.einsum("hrk,rhe->khe", score_grad, q_part.astype(jnp.float32)).reshape(
            patch_len, block * depth
        )
        value_grad = jnp.einsum(
            "hrk,rhe->khe", rounded, g_part, preferred_element_type=jnp.float32
        ).reshape(patch_len, block * depth)
        return (query_grad, key_grad, value_grad)

    query_parts, key_parts, value_parts = lax.map(backward_group, jnp.arange(groups))
    query_grad = regroup(query_parts).astype(jnp.bfloat16)
    key_sum, value_sum = (
        lax.psum_scatter(regroup(key_parts), "patch", scatter_dimension=0, tiled=True),
        lax.psum_scatter(regroup(value_parts), "patch", scatter_dimension=0, tiled=True),
    )
    key_grad = key_sum.astype(jnp.bfloat16)
    value_grad = value_sum.astype(jnp.bfloat16)
    packed_grad = jnp.concatenate([query_grad, key_grad, value_grad], axis=1)
    (path_grad,) = prep_pull(packed_grad)
    total_grad = residual_grad + path_grad
    return total_grad.reshape(points.shape)


def solution(mesh):
    in_specs = (
        P("curve", "patch", None, None),
        P(),
        P(),
        P(),
        P("curve", "patch", None),
        P(),
        P(),
        P(),
        P("patch", "curve", None),
        P("patch", "curve", None, None),
    )
    out_specs = P("curve", "patch", None, None)
    return jax.shard_map(shards, mesh=mesh, in_specs=in_specs, out_specs=out_specs, check_vma=False)
```

profile of v0, /device:TPU:6, one launch (start us, length us, event | category | flops | bytes accessed | tf_op | source)
XLA Modules:
  0.0 354.1 jit_solution(2144473138300720519)
XLA Ops:
  6.6 1.2 fusion.65
  9.0 2.1 convolution_convert_fusion.2
  12.3 1.4 scatter_custom_fusion
  14.4 17.8 %all-to-all-start = ((s32[128,1,4]{2,1,0:T(1,128)}), s32[128,1,4]{2,1,0:T(1,128)S(1)}, u32[]{:S(2)}, u32[]{:S(2)}) async-start(s32[128,1,4]{2,1,0:T(1,128)} %bitcast.21), calls=%async_computation | async-start | bytes 131072 | tf_op jit(solution)/shard_map/all_to_all | solution.py:128
  34.1 16.9 %all-gather.2.cloned.1.call-done = bf16[1024,1024]{1,0:T(8,128)(2,1)} async-done(((bf16[256,1024]{1,0:T(8,128)(2,1)}), bf16[1024,1024]{1,0:T(8,128)(2,1)}) %all-gather.2.cloned.1.call-update) | async-done | bytes 2097168 | tf_op jit(solution)/shard_map/all_gather | solution.py:84
  51.1 3.0 fusion.100
  54.0 1.5 copy.81
  55.5 2.3 copy.83
  58.5 40.3 %while.24 = (s32[]{:T(128)}, bf16[4,256,128]{1,2,0:T(8,128)(2,1)}, s32[4]{0:T(128)S(1)}, bf16[1024,512]{0,1:T(8,128)(2,1)S(1)}, bf16[256,512]{0,1:T(8,128)(2,1)}...) while((s32[]{:T(128)}, bf16[4,256,128]{1,2,0:T(8,128)(2,1)}, ...), condition=%wide.region_6.7_spmd, body=%wide.region_3.6_spmd.sunk | while | flops 139461632 | bytes 10363059 | solution.py:100
  61.6 3.3 fusion.159
  65.0 3.0 fusion.160
  71.7 3.4 fusion.159
  75.1 3.0 fusion.160
  81.8 3.3 fusion.159
  85.2 3.0 fusion.160
  91.9 3.4 fusion.159
  95.2 3.0 fusion.160
  98.9 2.1 fusion.43
  101.0 2.1 scatter_custom_fusion.1
  104.1 15.2 %all-to-all-start.1 = ((bf16[128,4,512]{2,1,0:T(4,128)(2,1)}), bf16[128,4,512]{2,1,0:T(4,128)(2,1)}, u32[]{:S(2)}, u32[]{:S(2)}) async-start(bf16[128,4,512]{2,1,0:T(4,128)(2,1)} %reshape.360), calls=%async_computation.1 | async-start | bytes 1048576 | tf_op jit(solution)/shard_map/all_to_all | solution.py:121
  120.0 1.1 copy.80
  122.9 15.1 %all-to-all-done.1 = bf16[128,4,512]{2,1,0:T(4,128)(2,1)} async-done(((bf16[128,4,512]{2,1,0:T(4,128)(2,1)}), bf16[128,4,512]{2,1,0:T(4,128)(2,1)}, u32[]{:S(2)}, u32[]{:S(2)}) %all-to-all-start.1) | async-done | bytes 524320 | tf_op jit(solution)/shard_map/all_to_all | solution.py:121
  138.0 2.0 reshape.406
  139.9 2.9 scatter_custom_fusion.2
  144.5 1.8 copy.85
  146.3 1.8 copy.84
  148.1 1.8 copy.87
  149.9 3.0 convolution_convert_fusion.3
  152.9 4.5 %fusion.102 = (f32[16,256]{1,0:T(8,128)S(1)}, f32[16,256,256]{1,2,0:T(8,128)}) fusion(pred[256,256]{0,1:T(8,128)(4,1)} %broadcast_compare_fusion, bf16[256,16,32]{0,2,1:T(8,128)(2,1)} %bitcast.185, bf16[256,16,32]{0,2,1:T(8,128)(2,1)} %bitcast.187), kind=kOutput, calls=%fused_computation.171 | convolution fusion | flops 71303424 | bytes 4800512 | tf_op jit(solution)/shard_map/jvp()/sub | solution.py:34
  157.5 4.0 %divide_convert_fusion.2 = (bf16[16,256,256]{1,2,0:T(8,128)(2,1)S(1)}, f32[16,256]{1,0:T(8,128)S(1)}) fusion(f32[16,256,256]{1,2,0:T(8,128)} %get-tuple-element.217, f32[16,256]{1,0:T(8,128)S(1)} %get-tuple-element.216, f32[16,256]{1,0:T(8,128)S(1)} %multiply_divide_fusion, bf16[16,256,256]{1,2,0:T(8,128)(2,1)} %convolution_convert_fusion.3), kind=kLoop, calls=%fused_computation.58 | loop fusion | flops 6287360 | bytes 8437760 | tf_op jit(solution)/shard_map/jvp()/convert_element_type | solution.py:35
  162.1 1.2 convolution_convert_fusion.7
  163.3 1.1 convolution_convert_fusion.8
  166.1 2.6 gather_fusion
  168.7 1.2 gather.10
  169.9 1.4 select_select_fusion
  171.2 7.5 %all-to-all-start.2 = ((bf16[128,4,512]{2,1,0:T(4,128)(2,1)}), bf16[128,4,512]{2,1,0:T(4,128)(2,1)}, u32[]{:S(2)}, u32[]{:S(2)}) async-start(bf16[128,4,512]{2,1,0:T(4,128)(2,1)} %select_select_fusion), calls=%async_computation.2 | async-start | bytes 1048576 | tf_op jit(solution)/shard_map/all_to_all | solution.py:152
  178.9 18.8 %all-to-all-done.2 = bf16[128,4,512]{2,1,0:T(4,128)(2,1)} async-done(((bf16[128,4,512]{2,1,0:T(4,128)(2,1)}), bf16[128,4,512]{2,1,0:T(4,128)(2,1)}, u32[]{:S(2)}, u32[]{:S(2)}) %all-to-all-start.2) | async-done | bytes 524320 | tf_op jit(solution)/shard_map/all_to_all | solution.py:152
  197.6 1.2 reshape.365
  198.8 1.9 gather_fusion.1
  200.6 2.1 convolution_convert_fusion.5
  203.5 74.5 %while.25 = (s32[]{:T(128)}, bf16[4,256,128]{1,2,0:T(8,128)(2,1)}, f32[4,1024,128]{1,2,0:T(8,128)}, f32[4,1024,128]{1,2,0:T(8,128)}, s32[4]{0:T(128)S(1)}, /*ind...) while((s32[]{:T(128)}, bf16[4,256,128]{1,2,0:T(8,128)(2,1)}, ...), condition=%wide.region_18.19_spmd, body=%wide.region_14.18_spmd.sunk | while | flops 356515840 | bytes 60391696 | solution.py:189
  206.6 2.1 convolution_convert_fusion.12
  209.6 3.3 fusion.171
  213.0 3.7 %fusion.172 = f32[4,256]{1,0:T(4,128)S(1)} fusion(bf16[4,256,1024]{2,1,0:T(8,128)(2,1)} %convolution_convert_fusion.12, f32[4,256,1024]{2,1,0:T(8,128)} %get-tuple-element.326, f32[4,256]{1,0:T(4,128)S(1)} %get-tuple-element.327), kind=kLoop, calls=%fused_computation.21.clone.1 | loop fusion | flops 4193280 | bytes 6299648 | tf_op jit(solution)/shard_map/while/body/eval_jaxpr/reduce_sum | solution.py:176
  219.9 1.2 fusion.175
  221.1 1.1 constant_dynamic-update-slice_fusion.9
  225.2 2.1 convolution_convert_fusion.12
  228.2 3.3 fusion.171
  231.6 3.7 %fusion.172 = f32[4,256]{1,0:T(4,128)S(1)} fusion(bf16[4,256,1024]{2,1,0:T(8,128)(2,1)} %convolution_convert_fusion.12, f32[4,256,1024]{2,1,0:T(8,128)} %get-tuple-element.326, f32[4,256]{1,0:T(4,128)S(1)} %get-tuple-element.327), kind=kLoop, calls=%fused_computation.21.clone.1 | loop fusion | flops 4193280 | bytes 6299648 | tf_op jit(solution)/shard_map/while/body/eval_jaxpr/reduce_sum | solution.py:176
  238.5 1.2 fusion.175
  239.7 1.1 constant_dynamic-update-slice_fusion.9
  243.9 2.1 convolution_convert_fusion.12
  246.9 3.4 fusion.171
  250.2 3.7 %fusion.172 = f32[4,256]{1,0:T(4,128)S(1)} fusion(bf16[4,256,1024]{2,1,0:T(8,128)(2,1)} %convolution_convert_fusion.12, f32[4,256,1024]{2,1,0:T(8,128)} %get-tuple-element.326, f32[4,256]{1,0:T(4,128)S(1)} %get-tuple-element.327), kind=kLoop, calls=%fused_computation.21.clone.1 | loop fusion | flops 4193280 | bytes 6299648 | tf_op jit(solution)/shard_map/while/body/eval_jaxpr/reduce_sum | solution.py:176
  257.1 1.2 fusion.175
  262.5 2.1 convolution_convert_fusion.12
  265.4 3.4 fusion.171
  268.8 3.7 %fusion.172 = f32[4,256]{1,0:T(4,128)S(1)} fusion(bf16[4,256,1024]{2,1,0:T(8,128)(2,1)} %convolution_convert_fusion.12, f32[4,256,1024]{2,1,0:T(8,128)} %get-tuple-element.326, f32[4,256]{1,0:T(4,128)S(1)} %get-tuple-element.327), kind=kLoop, calls=%fused_computation.21.clone.1 | loop fusion | flops 4193280 | bytes 6299648 | tf_op jit(solution)/shard_map/while/body/eval_jaxpr/reduce_sum | solution.py:176
  275.7 1.2 fusion.175
  276.9 1.1 constant_dynamic-update-slice_fusion.9
  278.8 26.7 %reduce-scatter.5.cloned.1.call-done = f32[256,512]{0,1:T(8,128)} async-done(((f32[1024,512]{0,1:T(8,128)}), f32[256,512]{0,1:T(8,128)}) %reduce-scatter.5.cloned.1.call-update) | async-done | bytes 524304 | tf_op jit(solution)/shard_map/reduce_scatter | solution.py:193
  305.5 1.1 convert_element_type.190
  306.6 36.8 %reduce-scatter.3.cloned.1.call-done = f32[256,512]{0,1:T(8,128)} async-done(((f32[1024,512]{0,1:T(8,128)}), f32[256,512]{0,1:T(8,128)}) %reduce-scatter.3.cloned.1.call-update) | async-done | bytes 524304 | tf_op jit(solution)/shard_map/reduce_scatter | solution.py:192
  344.5 2.1 fusion.68
  (157 shorter events, 56.2 us)
Async XLA Ops:
  6.5 136.4 %copy-start = (bf16[512,1536]{1,0:T(8,128)(2,1)S(1)}, bf16[512,1536]{1,0:T(8,128)(2,1)}, u32[]{:S(2)}) copy-start(bf16[512,1536]{1,0:T(8,128)(2,1)} %param.20) | copy-start | bytes 4718596
  6.5 5.5 %copy-start.18 = (s32[1,1,256]{2,1,0:T(1,128)S(1)}, s32[1,1,256]{2,1,0:T(1,128)}, u32[]{:S(2)}) copy-start(s32[1,1,256]{2,1,0:T(1,128)} %param.18) | copy-start | bytes 3076
  6.5 26.6 %copy-start.9 = (bf16[512,512]{1,0:T(8,128)(2,1)S(1)}, bf16[512,512]{1,0:T(8,128)(2,1)}, u32[]{:S(2)}) copy-start(bf16[512,512]{1,0:T(8,128)(2,1)} %param.21) | copy-start | bytes 1572868
  6.5 26.6 %copy-start.7 = (bf16[1,1,256,512]{3,2,1,0:T(8,128)(2,1)S(1)}, bf16[1,1,256,512]{3,2,1,0:T(8,128)(2,1)}, u32[]{:S(2)}) copy-start(bf16[1,1,256,512]{3,2,1,0:T(8,128)(2,1)} %param.23) | copy-start | bytes 786436
  6.5 44.5 %all-gather.2.cloned.1.call-start = ((), (), s32[]{:S(2)}) async-start(), calls=%async_computation.5 | async-start | bytes 2621440 | tf_op jit(solution)/shard_map/all_gather | solution.py:84
  7.8 0.6 copy-start.16
  8.4 0.6 copy-start.14
  14.4 89.6 %all-to-all-start = ((s32[128,1,4]{2,1,0:T(1,128)}), s32[128,1,4]{2,1,0:T(1,128)S(1)}, u32[]{:S(2)}, u32[]{:S(2)}) async-start(s32[128,1,4]{2,1,0:T(1,128)} %bitcast.21), calls=%async_computation | async-start | bytes 131072 | tf_op jit(solution)/shard_map/all_to_all | solution.py:128
  58.5 40.3 %copy-start.5 = (bf16[1,1,256,512]{3,2,1,0:T(8,128)(2,1)S(1)}, bf16[1,1,256,512]{3,2,1,0:T(8,128)(2,1)}, u32[]{:S(2)}) copy-start(bf16[1,1,256,512]{3,2,1,0:T(8,128)(2,1)} %param.14) | copy-start | bytes 786436
  58.5 60.7 %copy-start.19 = (s32[1,1,256]{2,1,0:T(1,128)S(1)}, s32[1,1,256]{2,1,0:T(1,128)}, u32[]{:S(2)}) copy-start(s32[1,1,256]{2,1,0:T(1,128)} %param.22) | copy-start | bytes 3076
  98.9 44.1 %copy-start.20 = (f32[512]{0:T(512)S(1)}, f32[512]{0:T(512)}, u32[]{:S(2)}) copy-start(f32[512]{0:T(512)} %param.19) | copy-start | bytes 6148
  104.1 33.9 %all-to-all-start.1 = ((bf16[128,4,512]{2,1,0:T(4,128)(2,1)}), bf16[128,4,512]{2,1,0:T(4,128)(2,1)}, u32[]{:S(2)}, u32[]{:S(2)}) async-start(bf16[128,4,512]{2,1,0:T(4,128)(2,1)} %reshape.360), calls=%async_computation.1 | async-start | bytes 1048576 | tf_op jit(solution)/shard_map/all_to_all | solution.py:121
  157.4 4.0 %copy-start.3 = (bf16[16,256,256]{1,2,0:T(8,128)(2,1)S(1)}, bf16[16,256,256]{1,2,0:T(8,128)(2,1)}, u32[]{:S(2)}) copy-start(bf16[16,256,256]{1,2,0:T(8,128)(2,1)} %convolution_convert_fusion.3) | copy-start | bytes 6291460
  157.4 4.7 %copy-start.4 = (f32[16,256,256]{1,2,0:T(8,128)S(1)}, f32[16,256,256]{1,2,0:T(8,128)}, u32[]{:S(2)}) copy-start(f32[16,256,256]{1,2,0:T(8,128)} %get-tuple-element.217) | copy-start | bytes 12582916
  157.4 4.7 %copy-start.11 = (bf16[256,512]{0,1:T(8,128)(2,1)S(1)}, bf16[256,512]{0,1:T(8,128)(2,1)}, u32[]{:S(2)}) copy-start(bf16[256,512]{0,1:T(8,128)(2,1)} %copy.85) | copy-start | bytes 786436
  157.4 4.7 %copy-start.13 = (pred[256,256]{0,1:T(8,128)(4,1)S(1)}, pred[256,256]{0,1:T(8,128)(4,1)}, u32[]{:S(2)}) copy-start(pred[256,256]{0,1:T(8,128)(4,1)} %broadcast_compare_fusion) | copy-start | bytes 196612
  162.1 1.2 copy-start.10
  164.4 1.5 copy-start.8
  171.2 26.4 %all-to-all-start.2 = ((bf16[128,4,512]{2,1,0:T(4,128)(2,1)}), bf16[128,4,512]{2,1,0:T(4,128)(2,1)}, u32[]{:S(2)}, u32[]{:S(2)}) async-start(bf16[128,4,512]{2,1,0:T(4,128)(2,1)} %select_select_fusion), calls=%async_computation.2 | async-start | bytes 1048576 | tf_op jit(solution)/shard_map/all_to_all | solution.py:152
  178.8 126.7 %reduce-scatter.5.cloned.1.call-start = ((), (), s32[]{:S(2)}) async-start(), calls=%async_computation.7 | async-start | bytes 2621440 | tf_op jit(solution)/shard_map/reduce_scatter | solution.py:193
  213.0 3.7 %copy-start.1 = (bf16[4,256,1024]{2,1,0:T(8,128)(2,1)S(1)}, bf16[4,256,1024]{2,1,0:T(8,128)(2,1)}, u32[]{:S(2)}) copy-start(bf16[4,256,1024]{2,1,0:T(8,128)(2,1)} %convolution_convert_fusion.12) | copy-start | bytes 6291460 | tf_op jit(solution)/shard_map/while
  213.0 4.7 %copy-start.2 = (f32[4,256,1024]{2,1,0:T(8,128)S(1)}, f32[4,256,1024]{2,1,0:T(8,128)}, u32[]{:S(2)}) copy-start(f32[4,256,1024]{2,1,0:T(8,128)} %get-tuple-element.326) | copy-start | bytes 12582916 | tf_op jit(solution)/shard_map/while
  231.6 3.7 %copy-start.1 = (bf16[4,256,1024]{2,1,0:T(8,128)(2,1)S(1)}, bf16[4,256,1024]{2,1,0:T(8,128)(2,1)}, u32[]{:S(2)}) copy-start(bf16[4,256,1024]{2,1,0:T(8,128)(2,1)} %convolution_convert_fusion.12) | copy-start | bytes 6291460 | tf_op jit(solution)/shard_map/while
  231.6 4.7 %copy-start.2 = (f32[4,256,1024]{2,1,0:T(8,128)S(1)}, f32[4,256,1024]{2,1,0:T(8,128)}, u32[]{:S(2)}) copy-start(f32[4,256,1024]{2,1,0:T(8,128)} %get-tuple-element.326) | copy-start | bytes 12582916 | tf_op jit(solution)/shard_map/while
  250.2 3.7 %copy-start.1 = (bf16[4,256,1024]{2,1,0:T(8,128)(2,1)S(1)}, bf16[4,256,1024]{2,1,0:T(8,128)(2,1)}, u32[]{:S(2)}) copy-start(bf16[4,256,1024]{2,1,0:T(8,128)(2,1)} %convolution_convert_fusion.12) | copy-start | bytes 6291460 | tf_op jit(solution)/shard_map/while
  250.2 4.7 %copy-start.2 = (f32[4,256,1024]{2,1,0:T(8,128)S(1)}, f32[4,256,1024]{2,1,0:T(8,128)}, u32[]{:S(2)}) copy-start(f32[4,256,1024]{2,1,0:T(8,128)} %get-tuple-element.326) | copy-start | bytes 12582916 | tf_op jit(solution)/shard_map/while
  268.8 3.7 %copy-start.1 = (bf16[4,256,1024]{2,1,0:T(8,128)(2,1)S(1)}, bf16[4,256,1024]{2,1,0:T(8,128)(2,1)}, u32[]{:S(2)}) copy-start(bf16[4,256,1024]{2,1,0:T(8,128)(2,1)} %convolution_convert_fusion.12) | copy-start | bytes 6291460 | tf_op jit(solution)/shard_map/while
  268.8 4.7 %copy-start.2 = (f32[4,256,1024]{2,1,0:T(8,128)S(1)}, f32[4,256,1024]{2,1,0:T(8,128)}, u32[]{:S(2)}) copy-start(f32[4,256,1024]{2,1,0:T(8,128)} %get-tuple-element.326) | copy-start | bytes 12582916 | tf_op jit(solution)/shard_map/while
  278.0 66.5 %copy-start.12 = (bf16[4,256,128]{1,2,0:T(8,128)(2,1)S(1)}, bf16[4,256,128]{1,2,0:T(8,128)(2,1)}, u32[]{:S(2)}) copy-start(bf16[4,256,128]{1,2,0:T(8,128)(2,1)} %get-tuple-element.87) | copy-start | bytes 786436
  278.0 66.5 %copy-start.21 = (f32[512]{0:T(512)S(1)}, f32[512]{0:T(512)}, u32[]{:S(2)}) copy-start(f32[512]{0:T(512)} %param.15) | copy-start | bytes 6148
  278.0 68.6 %copy-start.17 = (f32[256]{0:T(256)S(1)}, f32[256]{0:T(256)}, u32[]{:S(2)}) copy-start(f32[256]{0:T(256)} %copy-done.16) | copy-start | bytes 3076
  278.0 68.6 %copy-start.6 = (bf16[256,512]{1,0:T(8,128)(2,1)S(1)}, bf16[256,512]{1,0:T(8,128)(2,1)}, u32[]{:S(2)}) copy-start(bf16[256,512]{1,0:T(8,128)(2,1)} %gather_fusion.1) | copy-start | bytes 786436
  278.1 68.6 %copy-start.15 = (f32[256]{0:T(256)S(1)}, f32[256]{0:T(256)}, u32[]{:S(2)}) copy-start(f32[256]{0:T(256)} %copy-done.14) | copy-start | bytes 3076
  278.1 65.3 %reduce-scatter.3.cloned.1.call-start = ((), (), s32[]{:S(2)}) async-start(), calls=%async_computation.6 | async-start | bytes 2621440 | tf_op jit(solution)/shard_map/reduce_scatter | solution.py:192
Sparse Core Ops, SparseCore 0:
  12.1 38.8 all-gather.1
  278.2 27.2 reduce-scatter.4
  308.6 34.7 reduce-scatter.2
where the time goes:
time: 359 us; the launch traced here: 354 us
  waiting for transfers between devices  115 us (32%)
  matrix products  80.1 us (22%)
  local copies, waits for them, and re-layouts  73.3 us (20%)
  starting transfers between devices  40.7 us (11%)
  other arithmetic  26.5 us (7%)
  between operations  13.5 us (4%)
  loops' own time  5.05 us (1%)
    reduce_scatter x1, waiting for transfers between devices, shards(): lax.psum_scatter(regroup(key_parts), 'patch', scatter_dimension=0, tiled=...  36.8 us
    reduce_scatter x1, waiting for transfers between devices, shards(): lax.psum_scatter(regroup(value_parts), 'patch', scatter_dimension=0, tile...  26.7 us
    all_to_all x1, waiting for transfers between devices, shards(): lax.all_to_all(returning.reshape(curve_size, capacity, width), 'curve', s...  18.8 us
    dynamic_slice x28, local copies, waits for them, and re-layouts, head_view(): piece = lax.dynamic_slice_in_dim(matrix, index * columns, columns, 1)  18.6 us
    all_to_all x1, starting transfers between devices, shards(): lax.all_to_all(outgoing_at.reshape(curve_size, capacity), 'curve', split_...  17.8 us
    all_gather x1, waiting for transfers between devices, shards(): gathered = lax.all_gather(packed[:, width:], 'patch', axis=0, tiled=True)  16.9 us
    all_to_all x1, starting transfers between devices, shards(): lax.all_to_all(outgoing.reshape(curve_size, capacity, width), 'curve', sp...  15.2 us
    all_to_all x1, waiting for transfers between devices, shards(): lax.all_to_all(outgoing.reshape(curve_size, capacity, width), 'curve', sp...  15.1 us
  transfers between devices with their start and end apart: 6, of which 5 were waited for; matrix products, arithmetic and copies ran while one was open for 17% of the time, Pallas kernels for 0%

commit v1 on v0

v1 whole, which is shorter than its diff:
```python
import functools
import math

import jax
import jax.numpy as jnp
from jax import lax
from jax.experimental import pallas as pl
from jax.experimental.pallas import tpu as pltpu
from jax.sharding import PartitionSpec as P

HEADS = 16
EPS = 1e-06
F32 = jnp.float32
BF = jnp.bfloat16
MESH = pl.DeviceIdType.MESH
LANES = 128


def dot(a, b):
    return lax.dot_general(a, b, (((1,), (0,)), ((), ())), preferred_element_type=F32)


def dot_nt(a, b):
    return lax.dot_general(a, b, (((1,), (1,)), ((), ())), preferred_element_type=F32)


def dot_tn(a, b):
    return lax.dot_general(a, b, (((0,), (0,)), ((), ())), preferred_element_type=F32)


def iota(shape, dim):
    return lax.broadcasted_iota(jnp.int32, shape, dim)


def norm_scale(rows):
    return lax.rsqrt(jnp.mean(rows * rows, axis=-1, keepdims=True) + EPS)


def norm_grad(rows, gain, cot):
    r = norm_scale(rows)
    c = cot * gain
    inner = jnp.mean(c * rows, axis=-1, keepdims=True)
    return r * (c - rows * (r * r * inner))


def column(row, size):
    eye = iota((size, size), 0) == iota((size, size), 1)
    return jnp.sum(jnp.where(eye, row, 0.0), axis=1, keepdims=True)


def kernel(
    NP, NC, R, D, CAP, DEPTH,
    x_hbm, w1_hbm, o1_hbm, w2_hbm, o2_hbm, og_hbm, gain1, gain2, pos, seg,
    out,
    x, w1, o1, w2, o2, og,
    qkv_s, qkv_r, va, ex, inv_all, mix_all,
    mix_s, mix_r, at_s, at_r, tmp, a_s, a_r, b_s, b_r,
    pk, gat, p2, p2t, bias, hil, two, gtwo, dtwo,
    g_s, g_r, dq_acc, d_s, d_r,
    lsem, xs_sem, xr_sem, ms_sem, mr_sem, cs_sem, cr_sem, gs_sem, gr_sem, ds_sem, dr_sem,
):
    me_p = lax.axis_index("patch")
    me_c = lax.axis_index("curve")
    scale = DEPTH ** (-0.5)
    to_log2 = scale * math.log2(math.e)
    from_log2 = math.log(2.0)
    per = LANES // DEPTH
    KEYS = NP * R
    SLOTS = CAP * NC

    loads = [
        pltpu.make_async_copy(src, dst, lsem.at[i])
        for i, (src, dst) in enumerate(
            [(x_hbm, x), (w1_hbm, w1), (o1_hbm, o1), (w2_hbm, w2), (o2_hbm, o2), (og_hbm, og)]
        )
    ]
    for load in loads:
        load.start()

    barrier = pltpu.get_barrier_semaphore()

    def peer(k):
        return lax.rem(me_p + k, NP)

    for k in range(1, NP):
        pl.semaphore_signal(barrier, inc=1, device_id=(peer(k), me_c), device_id_type=MESH)

    @pl.loop(1, NC)
    def _(k):
        pl.semaphore_signal(
            barrier, inc=1, device_id=(me_p, lax.rem(me_c + k, NC)), device_id_type=MESH
        )

    def head_mask(rows, h):
        return iota((rows, LANES), 1) // DEPTH == h

    loads[0].wait()
    loads[1].wait()
    rows = x[...].astype(F32)
    normed = (rows * norm_scale(rows) * gain1[...]).astype(BF)
    for j in (1, 2, 0):
        part = dot(normed, w1[:, j * D : (j + 1) * D])
        part = (part * to_log2 if j == 0 else part).astype(BF)
        for p in range(NP):
            qkv_s[j, p] = part[:, p * LANES : (p + 1) * LANES]

    pl.semaphore_wait(barrier, NP - 1 + NC - 1)

    my_rows = pl.ds(pl.multiple_of(me_p * R, R), R)
    for j in (1, 2, 0):
        for k in range(1, NP):
            pltpu.make_async_remote_copy(
                src_ref=qkv_s.at[j, peer(k)],
                dst_ref=qkv_r.at[j, my_rows],
                send_sem=xs_sem,
                recv_sem=xr_sem.at[j],
                device_id=(peer(k), me_c),
                device_id_type=MESH,
            ).start()
        qkv_r[j, my_rows, :] = qkv_s[j, me_p]

    place = pos[...]
    owner_row = (place // R).astype(F32)
    offset_row = (place % R).astype(F32)
    owner_col = column(owner_row, R)
    offset_col = column(offset_row, R)
    same = owner_col == owner_row
    i0, i1 = iota((R, R), 0), iota((R, R), 1)
    rank_row = jnp.sum(jnp.where(same & (i0 < i1), 1.0, 0.0), axis=0, keepdims=True)
    rank_col = jnp.sum(jnp.where(same & (i1 < i0), 1.0, 0.0), axis=1, keepdims=True)
    slot_row = rank_row * NC + owner_row
    slot_col = rank_col * NC + owner_col
    pk[...] = jnp.where(iota((SLOTS, R), 0).astype(F32) == slot_row, 1.0, 0.0).astype(BF)
    gat[...] = jnp.where(iota((R, SLOTS), 1).astype(F32) == slot_col, 1.0, 0.0).astype(BF)
    table = dot(pk[...], jnp.broadcast_to(offset_col + 1.0, (R, LANES)).astype(BF))
    lane = iota((NC, LANES), 1)
    note = jnp.zeros((NC, LANES), F32)
    for r in range(CAP):
        note = jnp.where(lane == r, table[r * NC : (r + 1) * NC], note)
    at_s[...] = note.reshape(NC, 1, LANES)

    def spread(src, dst, send_sem, recv_sem):
        @pl.loop(1, NC)
        def _(k):
            other = lax.rem(me_c + k, NC)
            pltpu.make_async_remote_copy(
                src_ref=src.at[other],
                dst_ref=dst.at[me_c],
                send_sem=send_sem,
                recv_sem=recv_sem,
                device_id=(me_p, other),
                device_id_type=MESH,
            ).start()

        dst[me_c] = src[me_c]

    def wait_spread(buf, sem):
        part = buf.at[pl.ds(0, NC - 1)]
        pltpu.make_async_copy(part, part, sem).wait()

    spread(at_s, at_r, cs_sem.at[0], cr_sem.at[0])

    loads[4].wait()
    loads[5].wait()
    g2 = dot_nt(og[...], o2[...]).astype(BF)
    for g in range(NP):
        gtwo[g] = g2[:, g * LANES : (g + 1) * LANES]
    seg_row = seg[...].astype(F32)
    bias[...] = jnp.where(column(seg_row, R) == seg_row, 0.0, -1e30)

    def arrive(j):
        part = qkv_r.at[j, pl.ds(0, (NP - 1) * R)]
        pltpu.make_async_copy(part, part, xr_sem.at[j]).wait()

    arrive(1)
    arrive(2)
    va[:, :LANES] = qkv_r[2]
    va[:, LANES:] = jnp.ones((KEYS, LANES), BF)
    arrive(0)

    @pl.loop(0, NP)
    def _(k):
        s = lax.rem(me_p + 1 + k, NP)
        rows_s = pl.ds(pl.multiple_of(s * R, R), R)
        qs = qkv_r[0, rows_s, :]
        keys = qkv_r[1]
        mixed = jnp.zeros((R, LANES), F32)
        inv = jnp.zeros((R, LANES), F32)
        for h in range(per):
            mask = head_mask(R, h)
            scores = dot_nt(jnp.where(mask, qs, jnp.zeros((), BF)), keys)
            top = jnp.max(scores, axis=1, keepdims=True)
            e = jnp.exp2(scores - top).astype(BF)
            for t in range(NP):
                ex[h, t, rows_s, :] = e[:, t * R : (t + 1) * R]
            both = dot(e, va[...])
            one = 1.0 / both[:, LANES:]
            mixed = jnp.where(mask, both[:, :LANES] * one, mixed)
            inv = jnp.where(mask, one, inv)
        mix_all[rows_s, :] = mixed
        inv_all[rows_s, :] = inv
        mix_s[s] = mixed.astype(BF)

        @pl.when(k < NP - 1)
        def _():
            pltpu.make_async_remote_copy(
                src_ref=mix_s.at[s],
                dst_ref=mix_r.at[me_p],
                send_sem=ms_sem,
                recv_sem=mr_sem,
                device_id=(s, me_c),
                device_id_type=MESH,
            ).start()

    mix_r[me_p] = mix_s[me_p]

    wait_spread(at_r, cr_sem.at[0])
    landing = at_r[...].reshape(NC, LANES)
    turned = landing.T
    for r in range(CAP):
        p2[:, r * NC : (r + 1) * NC] = jnp.where(
            (iota((R, NC), 0) + 1).astype(F32) == turned[r : r + 1, :], 1.0, 0.0
        ).astype(BF)
        p2t[r * NC : (r + 1) * NC, :] = jnp.where(
            (iota((NC, R), 1) + 1).astype(F32) == landing[:, r : r + 1], 1.0, 0.0
        ).astype(BF)

    part = mix_r.at[pl.ds(0, NP - 1)]
    pltpu.make_async_copy(part, part, mr_sem).wait()
    loads[2].wait()
    mixed = jnp.concatenate([mix_r[p] for p in range(NP)], axis=1)
    moved = (x[...].astype(F32) + dot(mixed, o1[...])).astype(BF)

    chunks = D // LANES
    sub = CAP * chunks

    def pack(choose, what, dst):
        y = dot(choose, what)
        for r in range(CAP):
            for c in range(chunks):
                tmp[pl.ds(c * CAP + r, NC, sub), :] = y[
                    r * NC : (r + 1) * NC, c * LANES : (c + 1) * LANES
                ]
        dst[...] = tmp[...].reshape(NC, sub, LANES).astype(BF)

    def unpack(choose, src):
        tmp[...] = src[...].astype(F32).reshape(NC * sub, LANES)
        got = jnp.concatenate(
            [
                jnp.concatenate([tmp[pl.ds(c * CAP + r, NC, sub), :] for c in range(chunks)], axis=1)
                for r in range(CAP)
            ],
            axis=0,
        ).astype(BF)
        return dot(choose, got)

    pack(pk[...], moved, a_s)
    spread(a_s, a_r, cs_sem.at[1], cr_sem.at[1])
    loads[3].wait()
    wait_spread(a_r, cr_sem.at[1])

    hil[...] = unpack(p2[...], a_r)
    rows = hil[...]
    normed = (rows * norm_scale(rows) * gain2[...]).astype(BF)
    for j in range(3):
        part = dot(normed, w2[:, j * D : (j + 1) * D])
        part = (part * to_log2 if j == 0 else part).astype(BF)
        for g in range(NP):
            two[j, g] = part[:, g * LANES : (g + 1) * LANES]

    @pl.loop(0, NP)
    def _(g):
        qg, kg, vg, gg = two[0, g], two[1, g], two[2, g], gtwo[g].astype(F32)
        va2 = jnp.concatenate([vg, jnp.ones((R, LANES), BF)], axis=1)
        dq = jnp.zeros((R, LANES), F32)
        dk = jnp.zeros((R, LANES), F32)
        dv = jnp.zeros((R, LANES), F32)
        zero = jnp.zeros((), BF)
        for h in range(per):
            mask = head_mask(R, h)
            qh = jnp.where(mask, qg, zero)
            scores = dot_nt(qh, kg) + bias[...]
            e = jnp.exp2(scores - jnp.max(scores, axis=1, keepdims=True)).astype(BF)
            both = dot(e, va2)
            one = 1.0 / both[:, LANES:]
            gi = jnp.where(mask, gg * one, 0.0)
            inner = gi * (both[:, :LANES] * one)
            gib = gi.astype(BF)
            ga = jnp.concatenate([gib, (-inner).astype(BF)], axis=1)
            ds = (e.astype(F32) * dot_nt(ga, va2)).astype(BF)
            dq = dq + dot(ds, jnp.where(mask, kg, zero))
            dk = dk + dot_tn(ds, qh)
            dv = dv + dot_tn(e, gib)
        dtwo[0, g] = (dq * scale).astype(BF)
        dtwo[1, g] = (dk * from_log2).astype(BF)
        dtwo[2, g] = dv.astype(BF)

    def input_grad(d, w):
        total = None
        for j in range(3):
            piece = jnp.concatenate([d[j, g] for g in range(NP)], axis=1)
            term = dot_nt(piece, w[:, j * D : (j + 1) * D])
            total = term if total is None else total + term
        return total.astype(BF).astype(F32)

    path = norm_grad(hil[...], gain2[...], input_grad(dtwo, w2)).astype(BF)
    hil_grad = (og[...].astype(F32) + path.astype(F32)).astype(BF)

    pack(p2t[...], hil_grad, b_s)
    spread(b_s, b_r, cs_sem.at[2], cr_sem.at[2])
    wait_spread(b_r, cr_sem.at[2])
    moved_grad = unpack(gat[...], b_r).astype(BF)
    hil[...] = moved_grad.astype(F32)

    g1 = dot_nt(moved_grad, o1[...]).astype(BF)
    for p in range(NP):
        g_s[p] = g1[:, p * LANES : (p + 1) * LANES]
    for k in range(1, NP):
        pltpu.make_async_remote_copy(
            src_ref=g_s.at[peer(k)],
            dst_ref=g_r.at[my_rows],
            send_sem=gs_sem,
            recv_sem=gr_sem,
            device_id=(peer(k), me_c),
            device_id_type=MESH,
        ).start()
    g_r[my_rows, :] = g_s[me_p]
    part = g_r.at[pl.ds(0, (NP - 1) * R)]
    pltpu.make_async_copy(part, part, gr_sem).wait()

    dq_acc[...] = jnp.zeros((KEYS, LANES), F32)

    @pl.loop(0, NP)
    def _(k):
        t = lax.rem(me_p + 1 + k, NP)
        rows_t = pl.ds(pl.multiple_of(t * R, R), R)
        kt = qkv_r[1, rows_t, :]
        vat = va[rows_t, :]
        zero = jnp.zeros((), BF)
        dk = jnp.zeros((R, LANES), F32)
        dv = jnp.zeros((R, LANES), F32)
        gi = g_r[...].astype(F32) * inv_all[...]
        inner = (-gi * mix_all[...]).astype(BF)
        gi = gi.astype(BF)
        dq = dq_acc[...]
        for h in range(per):
            mask = head_mask(KEYS, h)
            gih = jnp.where(mask, gi, zero)
            ga = jnp.concatenate([gih, jnp.where(mask, inner, zero)], axis=1)
            e = ex[h, t]
            ds = (e.astype(F32) * dot_nt(ga, vat)).astype(BF)
            dq = dq + dot(ds, jnp.where(head_mask(R, h), kt, zero))
            dk = dk + dot_tn(ds, jnp.where(mask, qkv_r[0], zero))
            dv = dv + dot_tn(e, gih)
        dq_acc[...] = dq
        d_s[1, t] = (dk * from_log2).astype(BF)
        d_s[2, t] = dv.astype(BF)

        @pl.when(k < NP - 1)
        def _():
            for j in (1, 2):
                pltpu.make_async_remote_copy(
                    src_ref=d_s.at[j, t],
                    dst_ref=d_r.at[j, me_p],
                    send_sem=ds_sem,
                    recv_sem=dr_sem.at[j],
                    device_id=(t, me_c),
                    device_id_type=MESH,
                ).start()

    for p in range(NP):
        d_s[0, p] = (dq_acc[p * R : (p + 1) * R, :] * scale).astype(BF)
    for k in range(1, NP):
        pltpu.make_async_remote_copy(
            src_ref=d_s.at[0, peer(k)],
            dst_ref=d_r.at[0, me_p],
            send_sem=ds_sem,
            recv_sem=dr_sem.at[0],
            device_id=(peer(k), me_c),
            device_id_type=MESH,
        ).start()
    for j in range(3):
        d_r[j, me_p] = d_s[j, me_p]
    for j in (1, 2, 0):
        part = d_r.at[j, pl.ds(0, NP - 1)]
        pltpu.make_async_copy(part, part, dr_sem.at[j]).wait()

    path = norm_grad(x[...].astype(F32), gain1[...], input_grad(d_r, w1)).astype(BF)
    out[...] = (hil[...] + path.astype(F32)).astype(BF)

    for j in range(3):
        part = qkv_s.at[j, pl.ds(0, NP - 1)]
    part = qkv_s.at[:, pl.ds(0, NP - 1)]
    pltpu.make_async_copy(part, part, xs_sem).wait()
    part = mix_s.at[pl.ds(0, NP - 1)]
    pltpu.make_async_copy(part, part, ms_sem).wait()
    wait_spread(at_s, cs_sem.at[0])
    wait_spread(a_s, cs_sem.at[1])
    wait_spread(b_s, cs_sem.at[2])
    part = g_s.at[pl.ds(0, NP - 1)]
    pltpu.make_async_copy(part, part, gs_sem).wait()
    part = d_s.at[:, pl.ds(0, NP - 1)]
    pltpu.make_async_copy(part, part, ds_sem).wait()


def shards(
    points, norm_gain_one, qkv_one, out_one, hilbert_pos,
    norm_gain_two, qkv_two, out_two, hilbert_seg, out_grad,
):
    R, D = points.shape[2], points.shape[3]
    NP, NC = lax.axis_size("patch"), lax.axis_size("curve")
    DEPTH = D // HEADS
    CAP = 2 * R // NC
    KEYS, SLOTS, chunks = NP * R, CAP * NC, D // LANES
    per = LANES // DEPTH
    sub = CAP * chunks
    vmem = pl.BlockSpec(memory_space=pltpu.VMEM)
    hbm = pl.BlockSpec(memory_space=pl.ANY)
    V = pltpu.VMEM
    DMA = pltpu.SemaphoreType.DMA
    scratch = dict(
        x=V((R, D), BF), w1=V((D, 3 * D), BF), o1=V((D, D), BF), w2=V((D, 3 * D), BF),
        o2=V((D, D), BF), og=V((R, D), BF),
        qkv_s=V((3, NP, R, LANES), BF), qkv_r=V((3, KEYS, LANES), BF),
        va=V((KEYS, 2 * LANES), BF), ex=V((per, NP, KEYS, R), BF),
        inv_all=V((KEYS, LANES), F32), mix_all=V((KEYS, LANES), F32),
        mix_s=V((NP, R, LANES), BF), mix_r=V((NP, R, LANES), BF),
        at_s=V((NC, 1, LANES), F32), at_r=V((NC, 1, LANES), F32),
        tmp=V((NC * sub, LANES), F32),
        a_s=V((NC, sub, LANES), BF), a_r=V((NC, sub, LANES), BF),
        b_s=V((NC, sub, LANES), BF), b_r=V((NC, sub, LANES), BF),
        pk=V((SLOTS, R), BF), gat=V((R, SLOTS), BF), p2=V((R, SLOTS), BF), p2t=V((SLOTS, R), BF),
        bias=V((R, R), F32), hil=V((R, D), F32),
        two=V((3, NP, R, LANES), BF), gtwo=V((NP, R, LANES), BF), dtwo=V((3, NP, R, LANES), BF),
        g_s=V((NP, R, LANES), BF), g_r=V((KEYS, LANES), BF), dq_acc=V((KEYS, LANES), F32),
        d_s=V((3, NP, R, LANES), BF), d_r=V((3, NP, R, LANES), BF),
        lsem=DMA((6,)), xs=DMA, xr=DMA((3,)), ms=DMA, mr=DMA, cs=DMA((3,)), cr=DMA((3,)),
        gs=DMA, gr=DMA, ds=DMA, dr=DMA((3,)),
    )
    result = pl.pallas_call(
        functools.partial(kernel, NP, NC, R, D, CAP, DEPTH),
        out_shape=jax.ShapeDtypeStruct((R, D), BF),
        in_specs=[hbm] * 6 + [vmem] * 4,
        out_specs=vmem,
        scratch_shapes=list(scratch.values()),
        compiler_params=pltpu.CompilerParams(
            collective_id=0, has_side_effects=True, vmem_limit_bytes=56 * 1024 * 1024
        ),
    )(
        points.reshape(R, D), qkv_one, out_one, qkv_two, out_two, out_grad.reshape(R, D),
        norm_gain_one.reshape(1, D), norm_gain_two.reshape(1, D),
        hilbert_pos.reshape(1, R), hilbert_seg.reshape(1, R),
    )
    return result.reshape(points.shape)


def solution(mesh):
    in_specs = (
        P("curve", "patch", None, None), P(), P(), P(), P("curve", "patch", None),
        P(), P(), P(), P("patch", "curve", None), P("patch", "curve", None, None),
    )
    out_specs = P("curve", "patch", None, None)
    return jax.shard_map(shards, mesh=mesh, in_specs=in_specs, out_specs=out_specs, check_vma=False)
```

time: 359 us -> 110 us (0.31); the launches traced: 354 us -> 110 us
  waiting for transfers between devices: 115 us -> 0 us
  Pallas kernels: 0 us -> 108 us
  matrix products: 80.1 us -> 0 us
  local copies, waits for them, and re-layouts: 73.3 us -> 1.67 us
  starting transfers between devices: 40.7 us -> 0 us
  other arithmetic: 26.5 us -> 0 us
  between operations: 13.5 us -> 0.01 us
  loops' own time: 5.05 us -> 0 us
    pallas_call x0 -> x1, Pallas kernels: none -> 108 us  [shards(): pl.pallas_call(functools.partial(kernel, NP, NC, R, D, CAP, DEPTH), out_s...]
    reduce_scatter x2 -> x0, waiting for transfers between devices: 63.5 us -> none  [the longest x1 36.8 us: shards(): lax.psum_scatter(regroup(key_parts), 'patch', scatter_dimension=0, tiled=...]
    dot_general x32 -> x0, matrix products: 48.8 us -> none  [the longest x4 11.9 us: forward_group(): jnp.einsum('hrk,khe->rhe', weights, v_part, preferred_element_type=jnp.fl...]
    all_to_all x3 -> x0, starting transfers between devices: 40.5 us -> none  [the longest x1 17.8 us: shards(): lax.all_to_all(outgoing_at.reshape(curve_size, capacity), 'curve', split_...]
    all_to_all x3 -> x0, waiting for transfers between devices: 33.9 us -> none  [the longest x1 18.8 us: shards(): lax.all_to_all(returning.reshape(curve_size, capacity, width), 'curve', s...]
    sub x9 -> x0, matrix products: 31.3 us -> none  [the longest x4 13.4 us: forward_group(): weights = jax.nn.softmax(scores, axis=-1).astype(jnp.bfloat16)]
    dynamic_slice x36 -> x0, local copies, waits for them, and re-layouts: 23.2 us -> none  [the longest x28 18.6 us: head_view(): piece = lax.dynamic_slice_in_dim(matrix, index * columns, columns, 1)]
    all_gather x1 -> x0, waiting for transfers between devices: 16.9 us -> none  [shards(): gathered = lax.all_gather(packed[:, width:], 'patch', axis=0, tiled=True)]
  transfers between devices with their start and end apart: 6 -> 0, of which waited for: 5 -> 0; matrix products, arithmetic and copies ran while one was open for 17% -> 0% of each run, Pallas kernels for 0% -> 0%
where the time goes in v1:
time: 110 us
  Pallas kernels  108 us (98%)
  local copies, waits for them, and re-layouts  1.67 us (2%)
    pallas_call x1, Pallas kernels, shards(): pl.pallas_call(functools.partial(kernel, NP, NC, R, D, CAP, DEPTH), out_s...  108 us

profile of v1, /device:TPU:6, one launch (start us, length us, event | category | flops | bytes accessed | tf_op | source)
XLA Modules:
  0.0 109.6 jit_solution(12926500260069187242)
XLA Ops:
  0.0 107.9 %shard_map.100 = bf16[256,512]{1,0:T(8,128)(2,1)} custom-call(bf16[256,512]{1,0:T(8,128)(2,1)} %bitcast.8, bf16[512,1536]{1,0:T(8,128)(2,1)} %w1_hbm.1, bf16[512,512]{1,0:T(8,128)(2,1)} %o1_hbm.1, bf16[512,1536]{1,0:T(8,128)(2,1)} %w2_hbm.1, bf16[512,512]{1,0:T(8,128)(2,1)} %o2_hbm.1, bf16[256,512]{1,0:T(8,128)(2,1)} %bitcast.9, f32[1,512]{1,0:T(1,128)} %bitcast.10, ...), custom_call_target="tpu_custom_call" | custom-call | tf_op jit(solution)/shard_map/pallas_call | solution.py:440
  107.9 1.7 %copy.12 = bf16[1,1,256,512]{3,2,1,0:T(8,128)(2,1)} copy(bf16[1,1,256,512]{3,2,1,0:T(8,128)(2,1)} %bitcast.7) | data formatting | bytes 524288

commit v2 on v1

--- a/solution.py
+++ b/solution.py
@@ -56,8 +56,8 @@
     qkv_s, qkv_r, va, ex, inv_all, mix_all,
     mix_s, mix_r, at_s, at_r, tmp, a_s, a_r, b_s, b_r,
     pk, gat, p2, p2t, bias, hil, two, gtwo, dtwo,
-    g_s, g_r, dq_acc, d_s, d_r,
-    lsem, xs_sem, xr_sem, ms_sem, mr_sem, cs_sem, cr_sem, gs_sem, gr_sem, ds_sem, dr_sem,
+    g_s, g_r, dq_acc, d_s, d_r, qm, ga, dk_acc, dv_acc,
+    lsem, xs_sem, xr_sem, ms_sem, mr_sem, cs_sem, cr_sem, gs_sem, gr_sem, ds_sem, dr_sem, vouch_sem, xq_sem,
 ):
     me_p = lax.axis_index("patch")
     me_c = lax.axis_index("curve")
@@ -82,14 +82,27 @@
     def peer(k):
         return lax.rem(me_p + k, NP)
 
-    for k in range(1, NP):
-        pl.semaphore_signal(barrier, inc=1, device_id=(peer(k), me_c), device_id_type=MESH)
-
-    @pl.loop(1, NC)
-    def _(k):
-        pl.semaphore_signal(
-            barrier, inc=1, device_id=(me_p, lax.rem(me_c + k, NC)), device_id_type=MESH
-        )
+    inner = 1 << (NC.bit_length() // 2)
+    outer = NC // inner
+    row, place_in = me_c // inner, lax.rem(me_c, inner)
+    beside = [
+        (me_p, lax.rem(row + k, outer) * inner + place_in)
+        for k in ((1, outer - 1) if outer > 2 else (1,))
+    ]
+    greeted = [(peer(k), me_c) for k in range(1, NP)]
+    greeted += [(me_p, row * inner + lax.rem(place_in + k, inner)) for k in range(1, inner)]
+    greeted += beside
+    for device in greeted:
+        pl.semaphore_signal(barrier, inc=1, device_id=device, device_id_type=MESH)
+
+    def vouch(i):
+        for device in beside:
+            pl.semaphore_signal(vouch_sem.at[i], inc=1, device_id=device, device_id_type=MESH)
+
+    def vouched(i):
+        pl.semaphore_wait(vouch_sem.at[i], len(beside))
+
+    rounds = outer // 2
 
     def head_mask(rows, h):
         return iota((rows, LANES), 1) // DEPTH == h
@@ -104,20 +117,23 @@
         for p in range(NP):
             qkv_s[j, p] = part[:, p * LANES : (p + 1) * LANES]
 
-    pl.semaphore_wait(barrier, NP - 1 + NC - 1)
-
-    my_rows = pl.ds(pl.multiple_of(me_p * R, R), R)
+    pl.semaphore_wait(barrier, len(greeted))
+
+    def far(k):
+        return pl.ds((NP - k) % NP * R, R)
+
     for j in (1, 2, 0):
         for k in range(1, NP):
             pltpu.make_async_remote_copy(
                 src_ref=qkv_s.at[j, peer(k)],
-                dst_ref=qkv_r.at[j, my_rows],
+                dst_ref=qkv_r.at[j, far(k)],
                 send_sem=xs_sem,
-                recv_sem=xr_sem.at[j],
+                recv_sem=xr_sem.at[j] if j else xq_sem.at[NP - k],
                 device_id=(peer(k), me_c),
                 device_id_type=MESH,
             ).start()
-        qkv_r[j, my_rows, :] = qkv_s[j, me_p]
+        qkv_r[j, far(0), :] = qkv_s[j, me_p]
+    vouch(0)
 
     place = pos[...]
     owner_row = (place // R).astype(F32)
@@ -142,7 +158,7 @@
     def spread(src, dst, send_sem, recv_sem):
         @pl.loop(1, NC)
         def _(k):
-            other = lax.rem(me_c + k, NC)
+            other = lax.rem(me_c + lax.rem(k * 51, NC), NC)
             pltpu.make_async_remote_copy(
                 src_ref=src.at[other],
                 dst_ref=dst.at[me_c],
@@ -158,8 +174,6 @@
         part = buf.at[pl.ds(0, NC - 1)]
         pltpu.make_async_copy(part, part, sem).wait()
 
-    spread(at_s, at_r, cs_sem.at[0], cr_sem.at[0])
-
     loads[4].wait()
     loads[5].wait()
     g2 = dot_nt(og[...], o2[...]).astype(BF)
@@ -167,6 +181,12 @@
         gtwo[g] = g2[:, g * LANES : (g + 1) * LANES]
     seg_row = seg[...].astype(F32)
     bias[...] = jnp.where(column(seg_row, R) == seg_row, 0.0, -1e30)
+    for i in range(rounds):
+        vouched(i)
+        if i + 1 < rounds:
+            vouch(i + 1)
+    spread(at_s, at_r, cs_sem.at[0], cr_sem.at[0])
+
 
     def arrive(j):
         part = qkv_r.at[j, pl.ds(0, (NP - 1) * R)]
@@ -176,19 +196,25 @@
     arrive(2)
     va[:, :LANES] = qkv_r[2]
     va[:, LANES:] = jnp.ones((KEYS, LANES), BF)
-    arrive(0)
 
     @pl.loop(0, NP)
-    def _(k):
-        s = lax.rem(me_p + 1 + k, NP)
+    def _(s):
         rows_s = pl.ds(pl.multiple_of(s * R, R), R)
+
+        @pl.when(s > 0)
+        def _():
+            part = qkv_r.at[0, rows_s]
+            pltpu.make_async_copy(part, part, xq_sem.at[s]).wait()
+
         qs = qkv_r[0, rows_s, :]
         keys = qkv_r[1]
         mixed = jnp.zeros((R, LANES), F32)
         inv = jnp.zeros((R, LANES), F32)
         for h in range(per):
             mask = head_mask(R, h)
-            scores = dot_nt(jnp.where(mask, qs, jnp.zeros((), BF)), keys)
+            qh = jnp.where(mask, qs, jnp.zeros((), BF))
+            qm[h, rows_s, :] = qh
+            scores = dot_nt(qh, keys)
             top = jnp.max(scores, axis=1, keepdims=True)
             e = jnp.exp2(scores - top).astype(BF)
             for t in range(NP):
@@ -201,18 +227,18 @@
         inv_all[rows_s, :] = inv
         mix_s[s] = mixed.astype(BF)
 
-        @pl.when(k < NP - 1)
+        @pl.when(s > 0)
         def _():
             pltpu.make_async_remote_copy(
                 src_ref=mix_s.at[s],
                 dst_ref=mix_r.at[me_p],
                 send_sem=ms_sem,
                 recv_sem=mr_sem,
-                device_id=(s, me_c),
+                device_id=(peer(s), me_c),
                 device_id_type=MESH,
             ).start()
 
-    mix_r[me_p] = mix_s[me_p]
+    mix_r[me_p] = mix_s[0]
 
     wait_spread(at_r, cr_sem.at[0])
     landing = at_r[...].reshape(NC, LANES)
@@ -268,39 +294,36 @@
         for g in range(NP):
             two[j, g] = part[:, g * LANES : (g + 1) * LANES]
 
-    @pl.loop(0, NP)
-    def _(g):
-        qg, kg, vg, gg = two[0, g], two[1, g], two[2, g], gtwo[g].astype(F32)
+    def stack(m):
+        zero = jnp.zeros((), m.dtype)
+        return jnp.concatenate([jnp.where(head_mask(R, h), m, zero) for h in range(per)], axis=0)
+
+    for g in range(NP):
+        qg, kg, vg = stack(two[0, g]), two[1, g], two[2, g]
         va2 = jnp.concatenate([vg, jnp.ones((R, LANES), BF)], axis=1)
-        dq = jnp.zeros((R, LANES), F32)
-        dk = jnp.zeros((R, LANES), F32)
-        dv = jnp.zeros((R, LANES), F32)
-        zero = jnp.zeros((), BF)
-        for h in range(per):
-            mask = head_mask(R, h)
-            qh = jnp.where(mask, qg, zero)
-            scores = dot_nt(qh, kg) + bias[...]
-            e = jnp.exp2(scores - jnp.max(scores, axis=1, keepdims=True)).astype(BF)
-            both = dot(e, va2)
-            one = 1.0 / both[:, LANES:]
-            gi = jnp.where(mask, gg * one, 0.0)
-            inner = gi * (both[:, :LANES] * one)
-            gib = gi.astype(BF)
-            ga = jnp.concatenate([gib, (-inner).astype(BF)], axis=1)
-            ds = (e.astype(F32) * dot_nt(ga, va2)).astype(BF)
-            dq = dq + dot(ds, jnp.where(mask, kg, zero))
-            dk = dk + dot_tn(ds, qh)
-            dv = dv + dot_tn(e, gib)
+        scores = dot_nt(qg, kg) + jnp.concatenate([bias[...]] * per, axis=0)
+        e = jnp.exp2(scores - jnp.max(scores, axis=1, keepdims=True)).astype(BF)
+        both = dot(e, va2)
+        one = 1.0 / both[:, LANES:]
+        gi = stack(gtwo[g].astype(F32)) * one
+        less = -gi * (both[:, :LANES] * one)
+        gib = gi.astype(BF)
+        lhs = jnp.concatenate([gib, less.astype(BF)], axis=1)
+        ds = (e.astype(F32) * dot_nt(lhs, va2)).astype(BF)
+        full = dot(ds, kg)
+        dq = full[:R]
+        for h in range(1, per):
+            dq = jnp.where(head_mask(R, h), full[h * R : (h + 1) * R], dq)
         dtwo[0, g] = (dq * scale).astype(BF)
-        dtwo[1, g] = (dk * from_log2).astype(BF)
-        dtwo[2, g] = dv.astype(BF)
+        dtwo[1, g] = (dot_tn(ds, qg) * from_log2).astype(BF)
+        dtwo[2, g] = dot_tn(e, gib).astype(BF)
+
+    def input_term(d, w, j):
+        piece = jnp.concatenate([d[j, g] for g in range(NP)], axis=1)
+        return dot_nt(piece, w[:, j * D : (j + 1) * D])
 
     def input_grad(d, w):
-        total = None
-        for j in range(3):
-            piece = jnp.concatenate([d[j, g] for g in range(NP)], axis=1)
-            term = dot_nt(piece, w[:, j * D : (j + 1) * D])
-            total = term if total is None else total + term
+        total = input_term(d, w, 0) + input_term(d, w, 1) + input_term(d, w, 2)
         return total.astype(BF).astype(F32)
 
     path = norm_grad(hil[...], gain2[...], input_grad(dtwo, w2)).astype(BF)
@@ -318,78 +341,114 @@
     for k in range(1, NP):
         pltpu.make_async_remote_copy(
             src_ref=g_s.at[peer(k)],
-            dst_ref=g_r.at[my_rows],
+            dst_ref=g_r.at[far(k)],
             send_sem=gs_sem,
             recv_sem=gr_sem,
             device_id=(peer(k), me_c),
             device_id_type=MESH,
         ).start()
-    g_r[my_rows, :] = g_s[me_p]
+    g_r[far(0), :] = g_s[me_p]
+
+    def scaled(lo, count):
+        here = slice(lo, lo + count)
+        gi = g_r[here, :].astype(F32) * inv_all[here, :]
+        less = (-gi * mix_all[here, :]).astype(BF)
+        gi = gi.astype(BF)
+        zero = jnp.zeros((), BF)
+        for h in range(per):
+            mask = head_mask(count, h)
+            ga[h, here, :LANES] = jnp.where(mask, gi, zero)
+            ga[h, here, LANES:] = jnp.where(mask, less, zero)
+
+    def pair(lo, count, t):
+        here = slice(lo, lo + count)
+        rows_t = pl.ds(pl.multiple_of(t * R, R), R) if not isinstance(t, int) else pl.ds(t * R, R)
+        kt = qkv_r[1, rows_t, :]
+        vat = va[rows_t, :]
+        dq = dk = dv = None
+        for h in range(per):
+            gah = ga[h, here, :]
+            e = ex[h, t, here, :]
+            ds = (e.astype(F32) * dot_nt(gah, vat)).astype(BF)
+            q_term = dot(ds, jnp.where(head_mask(R, h), kt, jnp.zeros((), BF)))
+            k_term = dot_tn(ds, qm[h, here, :])
+            v_term = dot_tn(e, gah[:, :LANES])
+            dq = q_term if dq is None else dq + q_term
+            dk = k_term if dk is None else dk + k_term
+            dv = v_term if dv is None else dv + v_term
+        return dq, dk, dv
+
+    scaled(0, R)
+    dq_acc[...] = jnp.zeros((KEYS, LANES), F32)
+
+    @pl.loop(1, NP)
+    def _(t):
+        dq, dk, dv = pair(0, R, t)
+        dq_acc[:R] += dq
+        dk_acc[t] = dk
+        dv_acc[t] = dv
+
     part = g_r.at[pl.ds(0, (NP - 1) * R)]
     pltpu.make_async_copy(part, part, gr_sem).wait()
-
-    dq_acc[...] = jnp.zeros((KEYS, LANES), F32)
-
-    @pl.loop(0, NP)
-    def _(k):
-        t = lax.rem(me_p + 1 + k, NP)
-        rows_t = pl.ds(pl.multiple_of(t * R, R), R)
-        kt = qkv_r[1, rows_t, :]
-        vat = va[rows_t, :]
-        zero = jnp.zeros((), BF)
-        dk = jnp.zeros((R, LANES), F32)
-        dv = jnp.zeros((R, LANES), F32)
-        gi = g_r[...].astype(F32) * inv_all[...]
-        inner = (-gi * mix_all[...]).astype(BF)
-        gi = gi.astype(BF)
-        dq = dq_acc[...]
-        for h in range(per):
-            mask = head_mask(KEYS, h)
-            gih = jnp.where(mask, gi, zero)
-            ga = jnp.concatenate([gih, jnp.where(mask, inner, zero)], axis=1)
-            e = ex[h, t]
-            ds = (e.astype(F32) * dot_nt(ga, vat)).astype(BF)
-            dq = dq + dot(ds, jnp.where(head_mask(R, h), kt, zero))
-            dk = dk + dot_tn(ds, jnp.where(mask, qkv_r[0], zero))
-            dv = dv + dot_tn(e, gih)
-        dq_acc[...] = dq
-        d_s[1, t] = (dk * from_log2).astype(BF)
-        d_s[2, t] = dv.astype(BF)
-
-        @pl.when(k < NP - 1)
+    scaled(R, (NP - 1) * R)
+    dk_acc[0] = jnp.zeros((R, LANES), F32)
+    dv_acc[0] = jnp.zeros((R, LANES), F32)
+
+    @pl.loop(1, NP + 1)
+    def _(i):
+        t = lax.rem(i, NP)
+        dq, dk, dv = pair(R, (NP - 1) * R, t)
+        dq_acc[R:] += dq
+        dk = dk_acc[t] + dk
+        dv = dv_acc[t] + dv
+
+        @pl.when(i == NP)
         def _():
+            dk_acc[0] = dk
+            dv_acc[0] = dv
+
+        @pl.when(i < NP)
+        def _():
+            d_s[1, t] = (dk * from_log2).astype(BF)
+            d_s[2, t] = dv.astype(BF)
             for j in (1, 2):
                 pltpu.make_async_remote_copy(
                     src_ref=d_s.at[j, t],
                     dst_ref=d_r.at[j, me_p],
                     send_sem=ds_sem,
                     recv_sem=dr_sem.at[j],
-                    device_id=(t, me_c),
+                    device_id=(peer(t), me_c),
                     device_id_type=MESH,
                 ).start()
 
-    for p in range(NP):
-        d_s[0, p] = (dq_acc[p * R : (p + 1) * R, :] * scale).astype(BF)
     for k in range(1, NP):
+        d_s[0, k] = (dq_acc[k * R : (k + 1) * R, :] * scale).astype(BF)
         pltpu.make_async_remote_copy(
-            src_ref=d_s.at[0, peer(k)],
+            src_ref=d_s.at[0, k],
             dst_ref=d_r.at[0, me_p],
             send_sem=ds_sem,
             recv_sem=dr_sem.at[0],
             device_id=(peer(k), me_c),
             device_id_type=MESH,
         ).start()
-    for j in range(3):
-        d_r[j, me_p] = d_s[j, me_p]
-    for j in (1, 2, 0):
+
+    dq, dk, dv = pair(0, R, 0)
+    d_r[0, me_p] = ((dq_acc[:R] + dq) * scale).astype(BF)
+    d_r[1, me_p] = ((dk_acc[0] + dk) * from_log2).astype(BF)
+    d_r[2, me_p] = (dv_acc[0] + dv).astype(BF)
+
+    def landed(j):
         part = d_r.at[j, pl.ds(0, NP - 1)]
         pltpu.make_async_copy(part, part, dr_sem.at[j]).wait()
 
-    path = norm_grad(x[...].astype(F32), gain1[...], input_grad(d_r, w1)).astype(BF)
+    landed(1)
+    landed(2)
+    total = input_term(d_r, w1, 1) + input_term(d_r, w1, 2)
+    landed(0)
+    total = (total + input_term(d_r, w1, 0)).astype(BF).astype(F32)
+    path = norm_grad(x[...].astype(F32), gain1[...], total).astype(BF)
     out[...] = (hil[...] + path.astype(F32)).astype(BF)
 
-    for j in range(3):
-        part = qkv_s.at[j, pl.ds(0, NP - 1)]
     part = qkv_s.at[:, pl.ds(0, NP - 1)]
     pltpu.make_async_copy(part, part, xs_sem).wait()
     part = mix_s.at[pl.ds(0, NP - 1)]
@@ -434,8 +493,10 @@
         two=V((3, NP, R, LANES), BF), gtwo=V((NP, R, LANES), BF), dtwo=V((3, NP, R, LANES), BF),
         g_s=V((NP, R, LANES), BF), g_r=V((KEYS, LANES), BF), dq_acc=V((KEYS, LANES), F32),
         d_s=V((3, NP, R, LANES), BF), d_r=V((3, NP, R, LANES), BF),
+        qm=V((per, KEYS, LANES), BF), ga=V((per, KEYS, 2 * LANES), BF),
+        dk_acc=V((NP, R, LANES), F32), dv_acc=V((NP, R, LANES), F32),
         lsem=DMA((6,)), xs=DMA, xr=DMA((3,)), ms=DMA, mr=DMA, cs=DMA((3,)), cr=DMA((3,)),
-        gs=DMA, gr=DMA, ds=DMA, dr=DMA((3,)),
+        gs=DMA, gr=DMA, ds=DMA, dr=DMA((3,)), vouch=pltpu.SemaphoreType.REGULAR((8,)), xq=DMA((NP,)),
     )
     result = pl.pallas_call(
         functools.partial(kernel, NP, NC, R, D, CAP, DEPTH),

time: 110 us -> 95.3 us (0.87)
  Pallas kernels: 108 us -> 93.4 us
    pallas_call x1, Pallas kernels: 108 us -> 93.4 us  [shards(): pl.pallas_call(functools.partial(kernel, NP, NC, R, D, CAP, DEPTH), out_s...]
where the time goes in v2:
time: 95.3 us; the launch traced here: 95.1 us
  Pallas kernels  93.4 us (98%)
  local copies, waits for them, and re-layouts  1.67 us (2%)
    pallas_call x1, Pallas kernels, shards(): pl.pallas_call(functools.partial(kernel, NP, NC, R, D, CAP, DEPTH), out_s...  93.4 us

profile of v2, /device:TPU:6, one launch (start us, length us, event | category | flops | bytes accessed | tf_op | source)
XLA Modules:
  0.0 95.1 jit_solution(1759937137972919078)
XLA Ops:
  0.0 93.4 %shard_map.100 = bf16[256,512]{1,0:T(8,128)(2,1)} custom-call(bf16[256,512]{1,0:T(8,128)(2,1)} %bitcast.8, bf16[512,1536]{1,0:T(8,128)(2,1)} %w1_hbm.1, bf16[512,512]{1,0:T(8,128)(2,1)} %o1_hbm.1, bf16[512,1536]{1,0:T(8,128)(2,1)} %w2_hbm.1, bf16[512,512]{1,0:T(8,128)(2,1)} %o2_hbm.1, bf16[256,512]{1,0:T(8,128)(2,1)} %bitcast.9, f32[1,512]{1,0:T(1,128)} %bitcast.10, ...), custom_call_target="tpu_custom_call" | custom-call | tf_op jit(solution)/shard_map/pallas_call | solution.py:501
  93.4 1.7 %copy.12 = bf16[1,1,256,512]{3,2,1,0:T(8,128)(2,1)} copy(bf16[1,1,256,512]{3,2,1,0:T(8,128)(2,1)} %bitcast.7) | data formatting | bytes 524288

commit v3 on v2

--- a/solution.py
+++ b/solution.py
@@ -54,10 +54,10 @@
     out,
     x, w1, o1, w2, o2, og,
     qkv_s, qkv_r, va, ex, inv_all, mix_all,
-    mix_s, mix_r, at_s, at_r, tmp, a_s, a_r, b_s, b_r,
+    mix_s, mix_r, at_s, at_m, at_n, at_r, tmp, a_s, a_r, b_s, b_r,
     pk, gat, p2, p2t, bias, hil, two, gtwo, dtwo,
     g_s, g_r, dq_acc, d_s, d_r, qm, ga, dk_acc, dv_acc,
-    lsem, xs_sem, xr_sem, ms_sem, mr_sem, cs_sem, cr_sem, gs_sem, gr_sem, ds_sem, dr_sem, vouch_sem, xq_sem,
+    lsem, xs_sem, xr_sem, ms_sem, mr_sem, cs_sem, cr_sem, gs_sem, gr_sem, ds_sem, dr_sem, ns_sem, nr_sem, xq_sem,
 ):
     me_p = lax.axis_index("patch")
     me_c = lax.axis_index("curve")
@@ -68,14 +68,12 @@
     KEYS = NP * R
     SLOTS = CAP * NC
 
-    loads = [
-        pltpu.make_async_copy(src, dst, lsem.at[i])
-        for i, (src, dst) in enumerate(
-            [(x_hbm, x), (w1_hbm, w1), (o1_hbm, o1), (w2_hbm, w2), (o2_hbm, o2), (og_hbm, og)]
-        )
-    ]
-    for load in loads:
-        load.start()
+    thirds = [pl.ds(j * D, D) for j in range(3)]
+    moves = [(x_hbm, x)] + [(w1_hbm.at[:, thirds[j]], w1.at[:, thirds[j]]) for j in range(3)]
+    moves += [(o1_hbm, o1), (w2_hbm, w2), (o2_hbm, o2), (og_hbm, og)]
+    loads = [pltpu.make_async_copy(src, dst, lsem.at[i]) for i, (src, dst) in enumerate(moves)]
+    for i in (0, 2, 3, 1):
+        loads[i].start()
 
     barrier = pltpu.get_barrier_semaphore()
 
@@ -85,44 +83,29 @@
     inner = 1 << (NC.bit_length() // 2)
     outer = NC // inner
     row, place_in = me_c // inner, lax.rem(me_c, inner)
-    beside = [
-        (me_p, lax.rem(row + k, outer) * inner + place_in)
-        for k in ((1, outer - 1) if outer > 2 else (1,))
-    ]
     greeted = [(peer(k), me_c) for k in range(1, NP)]
     greeted += [(me_p, row * inner + lax.rem(place_in + k, inner)) for k in range(1, inner)]
-    greeted += beside
+    greeted += [(me_p, lax.rem(row + k, outer) * inner + place_in) for k in range(1, outer)]
     for device in greeted:
         pl.semaphore_signal(barrier, inc=1, device_id=device, device_id_type=MESH)
 
-    def vouch(i):
-        for device in beside:
-            pl.semaphore_signal(vouch_sem.at[i], inc=1, device_id=device, device_id_type=MESH)
-
-    def vouched(i):
-        pl.semaphore_wait(vouch_sem.at[i], len(beside))
-
-    rounds = outer // 2
-
     def head_mask(rows, h):
         return iota((rows, LANES), 1) // DEPTH == h
 
+    def far(k):
+        return pl.ds((NP - k) % NP * R, R)
+
     loads[0].wait()
-    loads[1].wait()
     rows = x[...].astype(F32)
     normed = (rows * norm_scale(rows) * gain1[...]).astype(BF)
     for j in (1, 2, 0):
+        loads[1 + j].wait()
         part = dot(normed, w1[:, j * D : (j + 1) * D])
         part = (part * to_log2 if j == 0 else part).astype(BF)
         for p in range(NP):
             qkv_s[j, p] = part[:, p * LANES : (p + 1) * LANES]
-
-    pl.semaphore_wait(barrier, len(greeted))
-
-    def far(k):
-        return pl.ds((NP - k) % NP * R, R)
-
-    for j in (1, 2, 0):
+        if j == 1:
+            pl.semaphore_wait(barrier, len(greeted))
         for k in range(1, NP):
             pltpu.make_async_remote_copy(
                 src_ref=qkv_s.at[j, peer(k)],
@@ -133,7 +116,8 @@
                 device_id_type=MESH,
             ).start()
         qkv_r[j, far(0), :] = qkv_s[j, me_p]
-    vouch(0)
+    for load in loads[4:]:
+        load.start()
 
     place = pos[...]
     owner_row = (place // R).astype(F32)
@@ -153,7 +137,22 @@
     note = jnp.zeros((NC, LANES), F32)
     for r in range(CAP):
         note = jnp.where(lane == r, table[r * NC : (r + 1) * NC], note)
-    at_s[...] = note.reshape(NC, 1, LANES)
+    for z in range(outer):
+        at_s[pl.ds(z, inner, outer), :] = note[z * inner : (z + 1) * inner]
+
+    def line(k, count, at):
+        return pl.ds(pl.multiple_of(lax.rem(at + k, count) * (NC // count), NC // count), NC // count)
+
+    for k in range(1, inner):
+        pltpu.make_async_remote_copy(
+            src_ref=at_s.at[line(k, inner, place_in)],
+            dst_ref=at_m.at[line(0, inner, place_in)],
+            send_sem=cs_sem.at[0],
+            recv_sem=cr_sem.at[0],
+            device_id=(me_p, row * inner + lax.rem(place_in + k, inner)),
+            device_id_type=MESH,
+        ).start()
+    at_m[line(0, inner, place_in), :] = at_s[line(0, inner, place_in), :]
 
     def spread(src, dst, send_sem, recv_sem):
         @pl.loop(1, NC)
@@ -174,19 +173,27 @@
         part = buf.at[pl.ds(0, NC - 1)]
         pltpu.make_async_copy(part, part, sem).wait()
 
-    loads[4].wait()
-    loads[5].wait()
+    loads[6].wait()
+    loads[7].wait()
     g2 = dot_nt(og[...], o2[...]).astype(BF)
     for g in range(NP):
         gtwo[g] = g2[:, g * LANES : (g + 1) * LANES]
     seg_row = seg[...].astype(F32)
     bias[...] = jnp.where(column(seg_row, R) == seg_row, 0.0, -1e30)
-    for i in range(rounds):
-        vouched(i)
-        if i + 1 < rounds:
-            vouch(i + 1)
-    spread(at_s, at_r, cs_sem.at[0], cr_sem.at[0])
-
+    part = at_m.at[pl.ds(0, (inner - 1) * outer)]
+    pltpu.make_async_copy(part, part, cr_sem.at[0]).wait()
+    for z in range(outer):
+        at_n[z * inner : (z + 1) * inner, :] = at_m[pl.ds(z, inner, outer), :]
+    for k in range(1, outer):
+        pltpu.make_async_remote_copy(
+            src_ref=at_n.at[line(k, outer, row)],
+            dst_ref=at_r.at[line(0, outer, row)],
+            send_sem=ns_sem,
+            recv_sem=nr_sem,
+            device_id=(me_p, lax.rem(row + k, outer) * inner + place_in),
+            device_id_type=MESH,
+        ).start()
+    at_r[line(0, outer, row), :] = at_n[line(0, outer, row), :]
 
     def arrive(j):
         part = qkv_r.at[j, pl.ds(0, (NP - 1) * R)]
@@ -240,20 +247,9 @@
 
     mix_r[me_p] = mix_s[0]
 
-    wait_spread(at_r, cr_sem.at[0])
-    landing = at_r[...].reshape(NC, LANES)
-    turned = landing.T
-    for r in range(CAP):
-        p2[:, r * NC : (r + 1) * NC] = jnp.where(
-            (iota((R, NC), 0) + 1).astype(F32) == turned[r : r + 1, :], 1.0, 0.0
-        ).astype(BF)
-        p2t[r * NC : (r + 1) * NC, :] = jnp.where(
-            (iota((NC, R), 1) + 1).astype(F32) == landing[:, r : r + 1], 1.0, 0.0
-        ).astype(BF)
-
     part = mix_r.at[pl.ds(0, NP - 1)]
     pltpu.make_async_copy(part, part, mr_sem).wait()
-    loads[2].wait()
+    loads[4].wait()
     mixed = jnp.concatenate([mix_r[p] for p in range(NP)], axis=1)
     moved = (x[...].astype(F32) + dot(mixed, o1[...])).astype(BF)
 
@@ -281,8 +277,21 @@
         return dot(choose, got)
 
     pack(pk[...], moved, a_s)
+    part = at_r.at[pl.ds(0, (outer - 1) * inner)]
+    pltpu.make_async_copy(part, part, nr_sem).wait()
     spread(a_s, a_r, cs_sem.at[1], cr_sem.at[1])
-    loads[3].wait()
+
+    landing = at_r[...]
+    turned = landing.T
+    for r in range(CAP):
+        p2[:, r * NC : (r + 1) * NC] = jnp.where(
+            (iota((R, NC), 0) + 1).astype(F32) == turned[r : r + 1, :], 1.0, 0.0
+        ).astype(BF)
+        p2t[r * NC : (r + 1) * NC, :] = jnp.where(
+            (iota((NC, R), 1) + 1).astype(F32) == landing[:, r : r + 1], 1.0, 0.0
+        ).astype(BF)
+
+    loads[5].wait()
     wait_spread(a_r, cr_sem.at[1])
 
     hil[...] = unpack(p2[...], a_r)
@@ -453,7 +462,10 @@
     pltpu.make_async_copy(part, part, xs_sem).wait()
     part = mix_s.at[pl.ds(0, NP - 1)]
     pltpu.make_async_copy(part, part, ms_sem).wait()
-    wait_spread(at_s, cs_sem.at[0])
+    part = at_s.at[pl.ds(0, (inner - 1) * outer)]
+    pltpu.make_async_copy(part, part, cs_sem.at[0]).wait()
+    part = at_n.at[pl.ds(0, (outer - 1) * inner)]
+    pltpu.make_async_copy(part, part, ns_sem).wait()
     wait_spread(a_s, cs_sem.at[1])
     wait_spread(b_s, cs_sem.at[2])
     part = g_s.at[pl.ds(0, NP - 1)]
@@ -484,7 +496,8 @@
         va=V((KEYS, 2 * LANES), BF), ex=V((per, NP, KEYS, R), BF),
         inv_all=V((KEYS, LANES), F32), mix_all=V((KEYS, LANES), F32),
         mix_s=V((NP, R, LANES), BF), mix_r=V((NP, R, LANES), BF),
-        at_s=V((NC, 1, LANES), F32), at_r=V((NC, 1, LANES), F32),
+        at_s=V((NC, LANES), F32), at_m=V((NC, LANES), F32),
+        at_n=V((NC, LANES), F32), at_r=V((NC, LANES), F32),
         tmp=V((NC * sub, LANES), F32),
         a_s=V((NC, sub, LANES), BF), a_r=V((NC, sub, LANES), BF),
         b_s=V((NC, sub, LANES), BF), b_r=V((NC, sub, LANES), BF),
@@ -495,8 +508,8 @@
         d_s=V((3, NP, R, LANES), BF), d_r=V((3, NP, R, LANES), BF),
         qm=V((per, KEYS, LANES), BF), ga=V((per, KEYS, 2 * LANES), BF),
         dk_acc=V((NP, R, LANES), F32), dv_acc=V((NP, R, LANES), F32),
-        lsem=DMA((6,)), xs=DMA, xr=DMA((3,)), ms=DMA, mr=DMA, cs=DMA((3,)), cr=DMA((3,)),
-        gs=DMA, gr=DMA, ds=DMA, dr=DMA((3,)), vouch=pltpu.SemaphoreType.REGULAR((8,)), xq=DMA((NP,)),
+        lsem=DMA((8,)), xs=DMA, xr=DMA((3,)), ms=DMA, mr=DMA, cs=DMA((3,)), cr=DMA((3,)),
+        gs=DMA, gr=DMA, ds=DMA, dr=DMA((3,)), ns=DMA, nr=DMA, xq=DMA((NP,)),
     )
     result = pl.pallas_call(
         functools.partial(kernel, NP, NC, R, D, CAP, DEPTH),

time: 95.3 us -> 95 us (level)
  no operation moved by 1% of the time
where the time goes in v3:
time: 95 us; the launch traced here: 94.7 us
  Pallas kernels  93.1 us (98%)
  local copies, waits for them, and re-layouts  1.67 us (2%)
    pallas_call x1, Pallas kernels, shards(): pl.pallas_call(functools.partial(kernel, NP, NC, R, D, CAP, DEPTH), out_s...  93.1 us

profile of v3, /device:TPU:6, one launch (start us, length us, event | category | flops | bytes accessed | tf_op | source)
XLA Modules:
  0.0 94.7 jit_solution(5713877628487725683)
XLA Ops:
  0.0 93.1 %shard_map.100 = bf16[256,512]{1,0:T(8,128)(2,1)} custom-call(bf16[256,512]{1,0:T(8,128)(2,1)} %bitcast.8, bf16[512,1536]{1,0:T(8,128)(2,1)} %w1_hbm.1, bf16[512,512]{1,0:T(8,128)(2,1)} %o1_hbm.1, bf16[512,1536]{1,0:T(8,128)(2,1)} %w2_hbm.1, bf16[512,512]{1,0:T(8,128)(2,1)} %o2_hbm.1, bf16[256,512]{1,0:T(8,128)(2,1)} %bitcast.9, f32[1,512]{1,0:T(1,128)} %bitcast.10, ...), custom_call_target="tpu_custom_call" | custom-call | tf_op jit(solution)/shard_map/pallas_call | solution.py:514
  93.1 1.7 %copy.12 = bf16[1,1,256,512]{3,2,1,0:T(8,128)(2,1)} copy(bf16[1,1,256,512]{3,2,1,0:T(8,128)(2,1)} %bitcast.7) | data formatting | bytes 524288

commit v4 on v3

--- a/solution.py
+++ b/solution.py
@@ -204,12 +204,10 @@
     va[:, :LANES] = qkv_r[2]
     va[:, LANES:] = jnp.ones((KEYS, LANES), BF)
 
-    @pl.loop(0, NP)
-    def _(s):
-        rows_s = pl.ds(pl.multiple_of(s * R, R), R)
-
-        @pl.when(s > 0)
-        def _():
+    for s in range(NP):
+        rows_s = pl.ds(s * R, R)
+
+        if s > 0:
             part = qkv_r.at[0, rows_s]
             pltpu.make_async_copy(part, part, xq_sem.at[s]).wait()
 
@@ -234,8 +232,7 @@
         inv_all[rows_s, :] = inv
         mix_s[s] = mixed.astype(BF)
 
-        @pl.when(s > 0)
-        def _():
+        if s > 0:
             pltpu.make_async_remote_copy(
                 src_ref=mix_s.at[s],
                 dst_ref=mix_r.at[me_p],
@@ -371,7 +368,7 @@
 
     def pair(lo, count, t):
         here = slice(lo, lo + count)
-        rows_t = pl.ds(pl.multiple_of(t * R, R), R) if not isinstance(t, int) else pl.ds(t * R, R)
+        rows_t = pl.ds(t * R, R)
         kt = qkv_r[1, rows_t, :]
         vat = va[rows_t, :]
         dq = dk = dv = None
@@ -390,8 +387,7 @@
     scaled(0, R)
     dq_acc[...] = jnp.zeros((KEYS, LANES), F32)
 
-    @pl.loop(1, NP)
-    def _(t):
+    for t in range(1, NP):
         dq, dk, dv = pair(0, R, t)
         dq_acc[:R] += dq
         dk_acc[t] = dk
@@ -403,21 +399,16 @@
     dk_acc[0] = jnp.zeros((R, LANES), F32)
     dv_acc[0] = jnp.zeros((R, LANES), F32)
 
-    @pl.loop(1, NP + 1)
-    def _(i):
-        t = lax.rem(i, NP)
+    for t in (*range(1, NP), 0):
         dq, dk, dv = pair(R, (NP - 1) * R, t)
         dq_acc[R:] += dq
         dk = dk_acc[t] + dk
         dv = dv_acc[t] + dv
 
-        @pl.when(i == NP)
-        def _():
+        if t == 0:
             dk_acc[0] = dk
             dv_acc[0] = dv
-
-        @pl.when(i < NP)
-        def _():
+        else:
             d_s[1, t] = (dk * from_log2).astype(BF)
             d_s[2, t] = dv.astype(BF)
             for j in (1, 2):

time: 95 us -> 94.7 us (level)
  no operation moved by 1% of the time
where the time goes in v4:
time: 94.7 us; the launch traced here: 94.5 us
  Pallas kernels  92.8 us (98%)
  local copies, waits for them, and re-layouts  1.67 us (2%)
    pallas_call x1, Pallas kernels, shards(): pl.pallas_call(functools.partial(kernel, NP, NC, R, D, CAP, DEPTH), out_s...  92.8 us

profile of v4, /device:TPU:6, one launch (start us, length us, event | category | flops | bytes accessed | tf_op | source)
XLA Modules:
  0.0 94.5 jit_solution(1608311901792235825)
XLA Ops:
  0.0 92.8 %shard_map.100 = bf16[256,512]{1,0:T(8,128)(2,1)} custom-call(bf16[256,512]{1,0:T(8,128)(2,1)} %bitcast.8, bf16[512,1536]{1,0:T(8,128)(2,1)} %w1_hbm.1, bf16[512,512]{1,0:T(8,128)(2,1)} %o1_hbm.1, bf16[512,1536]{1,0:T(8,128)(2,1)} %w2_hbm.1, bf16[512,512]{1,0:T(8,128)(2,1)} %o2_hbm.1, bf16[256,512]{1,0:T(8,128)(2,1)} %bitcast.9, f32[1,512]{1,0:T(1,128)} %bitcast.10, ...), custom_call_target="tpu_custom_call" | custom-call | tf_op jit(solution)/shard_map/pallas_call | solution.py:505
  92.8 1.7 %copy.12 = bf16[1,1,256,512]{3,2,1,0:T(8,128)(2,1)} copy(bf16[1,1,256,512]{3,2,1,0:T(8,128)(2,1)} %bitcast.7) | data formatting | bytes 524288

commit v5 on v3

--- a/solution.py
+++ b/solution.py
@@ -157,7 +157,10 @@
     def spread(src, dst, send_sem, recv_sem):
         @pl.loop(1, NC)
         def _(k):
-            other = lax.rem(me_c + lax.rem(k * 51, NC), NC)
+            turn = lax.rem(k * 37, NC)
+            there = lax.rem(row + turn // inner, outer) * inner
+            chip = lax.rem(place_in // 2 + lax.rem(turn, inner) // 2, inner // 2) * 2
+            other = there + chip + lax.rem(place_in + turn, 2)
             pltpu.make_async_remote_copy(
                 src_ref=src.at[other],
                 dst_ref=dst.at[me_c],
@@ -352,7 +355,7 @@
             src_ref=g_s.at[peer(k)],
             dst_ref=g_r.at[far(k)],
             send_sem=gs_sem,
-            recv_sem=gr_sem,
+            recv_sem=gr_sem.at[NP - k],
             device_id=(peer(k), me_c),
             device_id_type=MESH,
         ).start()
@@ -397,9 +400,10 @@
         dk_acc[t] = dk
         dv_acc[t] = dv
 
-    part = g_r.at[pl.ds(0, (NP - 1) * R)]
-    pltpu.make_async_copy(part, part, gr_sem).wait()
-    scaled(R, (NP - 1) * R)
+    for k in (1, *range(NP - 1, 1, -1)):
+        part = g_r.at[pl.ds(k * R, R)]
+        pltpu.make_async_copy(part, part, gr_sem.at[k]).wait()
+        scaled(k * R, R)
     dk_acc[0] = jnp.zeros((R, LANES), F32)
     dv_acc[0] = jnp.zeros((R, LANES), F32)
 
@@ -456,7 +460,7 @@
     landed(0)
     total = (total + input_term(d_r, w1, 0)).astype(BF).astype(F32)
     path = norm_grad(x[...].astype(F32), gain1[...], total).astype(BF)
-    out[...] = (hil[...] + path.astype(F32)).astype(BF)
+    out[...] = hil[...] + path.astype(F32)
 
     part = qkv_s.at[:, pl.ds(0, NP - 1)]
     pltpu.make_async_copy(part, part, xs_sem).wait()
@@ -509,11 +513,11 @@
         qm=V((per, KEYS, LANES), BF), ga=V((per, KEYS, 2 * LANES), BF),
         dk_acc=V((NP, R, LANES), F32), dv_acc=V((NP, R, LANES), F32),
         lsem=DMA((8,)), xs=DMA, xr=DMA((3,)), ms=DMA, mr=DMA, cs=DMA((3,)), cr=DMA((3,)),
-        gs=DMA, gr=DMA, ds=DMA, dr=DMA((3,)), ns=DMA, nr=DMA, xq=DMA((NP,)),
+        gs=DMA, gr=DMA((NP,)), ds=DMA, dr=DMA((3,)), ns=DMA, nr=DMA, xq=DMA((NP,)),
     )
     result = pl.pallas_call(
         functools.partial(kernel, NP, NC, R, D, CAP, DEPTH),
-        out_shape=jax.ShapeDtypeStruct((R, D), BF),
+        out_shape=jax.ShapeDtypeStruct((R, D), F32),
         in_specs=[hbm] * 6 + [vmem] * 4,
         out_specs=vmem,
         scratch_shapes=list(scratch.values()),
@@ -525,7 +529,7 @@
         norm_gain_one.reshape(1, D), norm_gain_two.reshape(1, D),
         hilbert_pos.reshape(1, R), hilbert_seg.reshape(1, R),
     )
-    return result.reshape(points.shape)
+    return result.astype(BF).reshape(points.shape)
 
 
 def solution(mesh):

time: 95 us -> 96.8 us (1.019)
  other arithmetic: 0 us -> 1.78 us
  Pallas kernels: 93.1 us -> 94.8 us
  local copies, waits for them, and re-layouts: 1.67 us -> 0 us
    reshape x0 -> x1, other arithmetic: none -> 1.78 us  [shards(): return result.astype(BF).reshape(points.shape)]
    pallas_call x1, Pallas kernels: 93.1 us -> 94.8 us  [shards(): pl.pallas_call(functools.partial(kernel, NP, NC, R, D, CAP, DEPTH), out_s...]
    unnamed x1 -> x0, local copies, waits for them, and re-layouts: 1.67 us -> none
where the time goes in v5:
time: 96.8 us; the launch traced here: 96.6 us
  Pallas kernels  94.8 us (98%)
  other arithmetic  1.78 us (2%)
    pallas_call x1, Pallas kernels, shards(): pl.pallas_call(functools.partial(kernel, NP, NC, R, D, CAP, DEPTH), out_s...  94.8 us

profile of v5, /device:TPU:6, one launch (start us, length us, event | category | flops | bytes accessed | tf_op | source)
XLA Modules:
  0.0 96.6 jit_solution(15321408650403065414)
XLA Ops:
  0.0 94.8 %shard_map.100 = f32[256,512]{1,0:T(8,128)} custom-call(bf16[256,512]{1,0:T(8,128)(2,1)} %bitcast.8, bf16[512,1536]{1,0:T(8,128)(2,1)} %w1_hbm.1, bf16[512,512]{1,0:T(8,128)(2,1)} %o1_hbm.1, bf16[512,1536]{1,0:T(8,128)(2,1)} %w2_hbm.1, bf16[512,512]{1,0:T(8,128)(2,1)} %o2_hbm.1, bf16[256,512]{1,0:T(8,128)(2,1)} %bitcast.9, f32[1,512]{1,0:T(1,128)} %bitcast.10, ...), custom_call_target="tpu_custom_call" | custom-call | tf_op jit(solution)/shard_map/pallas_call | solution.py:518
  94.8 1.8 %convert_bitcast_fusion = bf16[1,1,256,512]{3,2,1,0:T(8,128)(2,1)} fusion(f32[256,512]{1,0:T(8,128)} %shard_map.100), kind=kLoop, calls=%fused_computation | loop fusion | flops 131072 | bytes 786432 | tf_op jit(solution)/shard_map/reshape | solution.py:532
